TPU v7x, 512 devices: a whole 4x4x16 slice. The times are simulated.
512 devices in a mesh: dp: 64 (over z, x), tensor: 8 (over y, core).
Axes of the slice: x: 4, y: 4, z: 16, core: 2. Of those that a mesh axis runs over, the one named last changes fastest.
Arguments:
- grad_buckets: bfloat16 [8192, 57344], P(('tensor', 'dp')), may hold values from -33 to 33
- sketch: bfloat16 [8192, 512], P('tensor'), may hold values from -0.0625 to 0.0625
Outputs:
- basis_out: bfloat16 [512, 57344], P(None, ('dp', 'tensor'))
- projected: bfloat16 [512, 8192], P('dp', 'tensor')
All inputs are finite; a program needn't handle non-finite values.
Results may differ from a plain program's by a relative error of at most 0.0013.
Values may be sent and summed in bfloat16 or wider, within the bound.
A program may use at most 192 MiB of HBM per device.

v0:
```python
import math

import jax
import jax.numpy as jnp
from jax import lax
from jax.sharding import PartitionSpec as P


def gram_of(sketch_part):
    return jnp.dot(
        sketch_part,
        sketch_part.T,
        precision=lax.Precision.HIGHEST,
        preferred_element_type=jnp.float32,
    )


def shards(grad_buckets, sketch):
    dp_size = lax.axis_size("dp")
    local_rows = grad_buckets.shape[0]
    panel_width = grad_buckets.shape[1] // dp_size
    split_view = grad_buckets.reshape(local_rows, dp_size, panel_width)
    arrived = lax.all_to_all(split_view, "dp", split_axis=1, concat_axis=0, tiled=True)
    partial_sketch = lax.dot_general(
        sketch, arrived[:, 0, :], (((0,), (0,)), ((), ())), preferred_element_type=jnp.float32
    )
    arrived, partial_sketch = (arrived, partial_sketch[:, None, :])
    grad_panel = arrived[:, 0, :]
    sketch_piece = lax.psum_scatter(
        partial_sketch[:, 0, :], "tensor", scatter_dimension=1, tiled=True
    )
    gram_matrix = lax.psum(gram_of(sketch_piece), ("dp", "tensor"))
    lower_factor = jnp.linalg.cholesky(gram_matrix)
    basis_piece = jax.scipy.linalg.solve_triangular(lower_factor, sketch_piece, lower=True)
    basis_out = (basis_piece * math.sqrt(panel_width * dp_size)).astype(jnp.bfloat16)
    matching = grad_panel.astype(jnp.float32)
    folded = lax.dot_general(
        lax.all_gather(basis_piece, "tensor", axis=1, tiled=True),
        matching,
        (((1,), (1,)), ((), ())),
        precision=lax.Precision.HIGHEST,
        preferred_element_type=jnp.float32,
    )
    projected = lax.psum_scatter(folded, "dp", scatter_dimension=0, tiled=True)
    return (basis_out, projected.astype(jnp.bfloat16))


def solution(mesh):
    in_specs = (P(("tensor", "dp"), None), P("tensor", None))
    out_specs = (P(None, ("dp", "tensor")), P("dp", "tensor"))
    return jax.shard_map(shards, mesh=mesh, in_specs=in_specs, out_specs=out_specs, check_vma=False)
```

profile of v0, /device:TPU:24, one launch (start us, length us, event | category | flops | bytes accessed | tf_op | source)
XLA Modules:
  0.0 1508.7 jit_solution(8544421798995677620)
XLA Ops:
  7.2 1.7 copy.17
  9.0 107.4 %all_to_all.15 = bf16[16,64,896]{2,0,1:T(8,128)(2,1)S(1)} all-to-all(bf16[16,64,896]{2,0,1:T(8,128)(2,1)S(1)} %bitcast.63), channel_id=1, replica_groups=mesh['dp'=64,'tensor'=8] {'dp'}, dimensions={1} | all-to-all | bytes 3670016 | tf_op jit(solution)/shard_map/all_to_all | solution.py:23
  117.6 2.4 fusion.31
  120.0 29.1 %reduce-scatter.3.cloned.1.call-done = f32[512,112]{0,1:T(8,128)} async-done(((f32[512,896]{0,1:T(8,128)}), f32[512,112]{0,1:T(8,128)}) %reduce-scatter.3.cloned.1.call-update) | async-done | bytes 229392 | tf_op jit(solution)/shard_map/reduce_scatter | solution.py:29
  149.2 3.1 fusion.32
  152.5 470.6 %all-reduce.3.cloned.1.call-done = f32[512,512]{0,1:T(8,128)} async-done(((f32[512,512]{0,1:T(8,128)}), f32[512,512]{0,1:T(8,128)}) %all-reduce.3.cloned.1.call-update) | async-done | bytes 1048592 | tf_op jit(solution)/shard_map/psum | solution.py:32
  623.1 1.6 copy.13
  626.0 11.7 cholesky.104
  637.7 9.8 custom-call.31
  650.2 11.7 cholesky.217
  662.0 10.0 custom-call.32
  673.5 11.7 cholesky.238
  686.0 9.8 custom-call.33
  697.2 11.7 cholesky.255
  713.2 10.9 while.1
  713.9 2.0 bitcast_dynamic-update-slice_fusion.2
  716.6 2.0 bitcast_dynamic-update-slice_fusion.2
  719.3 2.1 bitcast_dynamic-update-slice_fusion.2
  722.1 2.0 bitcast_dynamic-update-slice_fusion.2
  724.1 40.1 %custom-call.34 = f32[4,128,128]{1,2,0:T(8,128)S(1)} custom-call(f32[4,128,128]{2,1,0:T(8,128)} %get-tuple-element.9), custom_call_target="InvertDiagBlocksLowerTriangular" | custom-call | tf_op jit(solution)/shard_map/jit(_solve_triangular)/triangular_solve | solution.py:34
  766.8 29.0 %all-gather.2.cloned.1.call-done = f32[512,896]{0,1:T(8,128)} async-done(((f32[512,112]{0,1:T(8,128)}), f32[512,896]{0,1:T(8,128)}) %all-gather.2.cloned.1.call-update) | async-done | bytes 1835024 | tf_op jit(solution)/shard_map/all_gather | solution.py:38
  795.9 9.3 fusion.33
  805.2 695.1 %reduce-scatter.5.cloned.1.call-done = f32[8,1024]{1,0:T(8,128)} async-done(((f32[512,1024]{1,0:T(8,128)}), f32[8,1024]{1,0:T(8,128)}) %reduce-scatter.5.cloned.1.call-update) | async-done | bytes 32784 | tf_op jit(solution)/shard_map/reduce_scatter | solution.py:44
  1500.4 1.4 convert_element_type.8
  (56 shorter events, 16.1 us)
Async XLA Ops:
  7.2 110.4 %copy-start = (bf16[1024,512]{1,0:T(8,128)(2,1)S(1)}, bf16[1024,512]{1,0:T(8,128)(2,1)}, u32[]{:S(2)}) copy-start(bf16[1024,512]{1,0:T(8,128)(2,1)} %param.3) | copy-start | bytes 3145732
  7.2 142.0 %reduce-scatter.3.cloned.1.call-start = ((), (), s32[]{:S(2)}) async-start(), calls=%async_computation.3 | async-start | bytes 2064384 | tf_op jit(solution)/shard_map/reduce_scatter | solution.py:29
  116.3 1.2 copy-start.4
  120.0 503.1 %all-reduce.3.cloned.1.call-start = ((), (), s32[]{:S(2)}) async-start(), calls=%async_computation.4 | async-start | bytes 2097152 | tf_op jit(solution)/shard_map/psum | solution.py:32
  152.3 643.6 %all-gather.2.cloned.1.call-start = ((), (), s32[]{:S(2)}) async-start(), calls=%async_computation.5 | async-start | bytes 2064384 | tf_op jit(solution)/shard_map/all_gather | solution.py:38
  623.1 1.7 copy-start.1
  625.0 1.0 copy-start.2
  685.3 79.0 %copy-start.3 = (f32[512,112]{0,1:T(8,128)S(1)}, f32[512,112]{0,1:T(8,128)}, u32[]{:S(2)}) copy-start(f32[512,112]{0,1:T(8,128)} %reduce-scatter.3.cloned.1.call-done) | copy-start | bytes 688132
  766.8 733.6 %reduce-scatter.5.cloned.1.call-start = ((), (), s32[]{:S(2)}) async-start(), calls=%async_computation.6 | async-start | bytes 2129920 | tf_op jit(solution)/shard_map/reduce_scatter | solution.py:44
Sparse Core Ops, SparseCore 0:
  120.1 29.0 reduce-scatter.2
  154.6 468.4 all-reduce.2
  766.9 28.9 all-gather.1
  805.3 694.9 reduce-scatter.4
where the time goes:
time: 1510 us
  waiting for transfers between devices  1220 us (81%)
  other arithmetic  121 us (8%)
  blocking collectives  107 us (7%)
  matrix products  22 us (1%)
  between operations  17 us (1%)
  local copies, waits for them, and re-layouts  16.6 us (1%)
    reduce_scatter x1, waiting for transfers between devices, shards(): projected = lax.psum_scatter(folded, 'dp', scatter_dimension=0, tiled=True)  695 us
    psum x1, waiting for transfers between devices, shards(): gram_matrix = lax.psum(gram_of(sketch_piece), ('dp', 'tensor'))  471 us
    all_to_all x1, blocking collectives, shards(): lax.all_to_all(split_view, 'dp', split_axis=1, concat_axis=0, tiled=True)  107 us
    another operation x14, other arithmetic, shards(): lower_factor = jnp.linalg.cholesky(gram_matrix)  78.6 us
    another operation x4, other arithmetic, shards(): jax.scipy.linalg.solve_triangular(lower_factor, sketch_piece, lower=True)  41.2 us
  transfers between devices with their start and end apart: 4, of which 4 were waited for; matrix products, arithmetic and copies ran while one was open for 0% of the time, Pallas kernels for 0%

commit v1 on v0

v1 whole, which is shorter than its diff:
```python
import math

import jax
import jax.numpy as jnp
from jax import lax
from jax.experimental import pallas as pl
from jax.experimental.pallas import tpu as pltpu
from jax.sharding import PartitionSpec as P

MESH = pl.DeviceIdType.MESH
F32 = jnp.float32
BF16 = jnp.bfloat16
NZ, NX, NT = 16, 4, 8
NM = NX * NT
ROWS = 57344
RANK = 512
WIDE = 16
BLK = ROWS // (NZ * NM)
COLS = BLK * NZ
PW = WIDE * NM
HALF = RANK // 2
CHUNK = 256
TDOT = (((0,), (0,)), ((), ()))


def mod(a, n):
    return lax.rem(a + n, n)


def comm_kernel(
    packed, s_piece, gall_out, rhs_out,
    recv_b, recv_s, ypart, yall, rup, rdn, wpart, wrecv, gpart, grecv, gz,
    local_sem, a2a_send, a2a_recv, s_send, s_recv, rs_send, rs_recv, ag_send, ag_recv,
    g_send, g_recv, w_send, w_recv, gz_send, gz_recv, gp_send, gp_recv,
):
    dp = lax.axis_index("dp")
    t = lax.axis_index("tensor")
    z = dp // NX
    x = dp % NX
    m = x * NT + t
    chip = m // 2
    core = m % 2

    def member(i):
        return (z * NX + i // NT, i % NT)

    def at_z(i):
        return (i * NX + x, t)

    zup, zdn = at_z(mod(z + 1, NZ)), at_z(mod(z - 1, NZ))

    barrier = pltpu.get_barrier_semaphore()

    @pl.loop(1, NM)
    def _(k):
        pl.semaphore_signal(barrier, inc=1, device_id=member((m + k) % NM), device_id_type=MESH)

    @pl.loop(1, NZ)
    def _(k):
        pl.semaphore_signal(barrier, inc=1, device_id=at_z((z + k) % NZ), device_id_type=MESH)

    pl.semaphore_wait(barrier, NM - 1 + NZ - 1)

    def b_copy(k):
        peer = (m + k) % NM
        return pltpu.make_async_remote_copy(
            src_ref=packed.at[peer], dst_ref=recv_b.at[pl.ds(pl.multiple_of(m * WIDE, WIDE), WIDE)],
            send_sem=a2a_send.at[k], recv_sem=a2a_recv.at[k], device_id=member(peer), device_id_type=MESH,
        )

    def s_copy(k):
        peer = (t + k) % NT
        return pltpu.make_async_remote_copy(
            src_ref=s_piece, dst_ref=recv_s.at[:, t],
            send_sem=s_send.at[k], recv_sem=s_recv.at[k], device_id=(dp, peer), device_id_type=MESH,
        )

    @pl.loop(1, NT)
    def _(k):
        s_copy(k).start()

    @pl.loop(1, NM)
    def _(k):
        b_copy(k).start()

    own_b = pltpu.make_async_copy(
        packed.at[m], recv_b.at[pl.ds(pl.multiple_of(m * WIDE, WIDE), WIDE)], local_sem.at[0])
    own_s = pltpu.make_async_copy(s_piece, recv_s.at[:, t], local_sem.at[1])
    own_b.start()
    own_s.start()
    own_b.wait()
    own_s.wait()

    @pl.loop(1, NT)
    def _(k):
        s_copy(k).wait()

    @pl.loop(1, NM)
    def _(k):
        b_copy(k).wait()

    @pl.loop(0, COLS // CHUNK)
    def _(i):
        rows = pl.ds(pl.multiple_of(i * CHUNK, CHUNK), CHUNK)
        ypart[rows, :] = lax.dot_general(
            recv_b[:, rows], recv_s[...].reshape(PW, RANK), TDOT, preferred_element_type=F32)

    def block(b):
        return pl.ds(pl.multiple_of(mod(b, NZ) * BLK, 8), BLK)

    halves = (pl.ds(0, HALF), pl.ds(HALF, HALF))
    chains = ((0, 1, 0, 0), (1, -1, 1, 0), (2, 1, 1, 1), (3, -1, 0, 1))

    def rs_copy(chain, s, src):
        name, way, h, _ = chain
        buf = rup if way == 1 else rdn
        return pltpu.make_async_remote_copy(
            src_ref=src, dst_ref=buf.at[s, :, halves[h]],
            send_sem=rs_send.at[name, s], recv_sem=rs_recv.at[name, s],
            device_id=zup if way == 1 else zdn, device_id_type=MESH,
        )

    def rs_first(chain):
        _, way, h, s = chain
        rs_copy(chain, s, ypart.at[block(z + way * (8 - s)), halves[h]]).start()

    def rs_next(chain, s):
        _, way, h, _ = chain
        buf = rup if way == 1 else rdn
        slot = buf.at[s - 1, :, halves[h]]
        rs_copy(chain, s - 1, slot).wait_recv()
        buf[s - 1, :, halves[h]] += ypart[block(z + way * (8 - s)), halves[h]]
        rs_copy(chain, s, slot).start()

    for chain in chains:
        rs_first(chain)
    for chain in chains[:2]:
        rs_next(chain, 1)

    @pl.loop(2, 8)
    def _(s):
        for chain in chains:
            rs_next(chain, s)

    own = block(z)
    for chain in chains:
        _, way, h, _ = chain
        rs_copy(chain, 7, (rup if way == 1 else rdn).at[7, :, halves[h]]).wait_recv()
    yall[own, :] = ypart[own, :] + rup[7] + rdn[7]

    def ag_copy(chain, s):
        name, way, h, _ = chain
        piece = yall.at[block(z - way * s), halves[h]]
        return pltpu.make_async_remote_copy(
            src_ref=piece, dst_ref=piece, send_sem=ag_send.at[name, s], recv_sem=ag_recv.at[name, s],
            device_id=zup if way == 1 else zdn, device_id_type=MESH,
        )

    def ag_arrived(chain, s):
        name, way, h, _ = chain
        piece = yall.at[block(z - way * (s + 1)), halves[h]]
        pltpu.make_async_remote_copy(
            src_ref=piece, dst_ref=piece, send_sem=ag_send.at[name, s], recv_sem=ag_recv.at[name, s],
            device_id=zup if way == 1 else zdn, device_id_type=MESH,
        ).wait_recv()

    for chain in chains:
        ag_copy(chain, 0).start()
    rhs_out[pl.ds(0, BLK), :] = yall[own, :]

    @pl.loop(1, 7)
    def _(s):
        for chain in chains:
            ag_arrived(chain, s - 1)
            ag_copy(chain, s).start()

    for chain in chains[:2]:
        ag_arrived(chain, 6)
        ag_copy(chain, 7).start()
    for chain in chains[2:]:
        ag_arrived(chain, 6)
    for chain in chains[:2]:
        ag_arrived(chain, 7)

    gcols = pl.ds(pl.multiple_of((z // 4) * 128, 128), 128)
    gpart[...] = jnp.zeros_like(gpart)

    @pl.loop(0, COLS // CHUNK)
    def _(i):
        rows = pl.ds(pl.multiple_of(i * CHUNK, CHUNK), CHUNK)
        y = yall[rows, :]
        hi = y.astype(BF16)
        lo = (y - hi.astype(F32)).astype(BF16)
        ys = yall[rows, gcols]
        shi = ys.astype(BF16)
        slo = (ys - shi.astype(F32)).astype(BF16)
        gpart[...] += (
            lax.dot_general(shi, hi, TDOT, preferred_element_type=F32)
            + (lax.dot_general(shi, lo, TDOT, preferred_element_type=F32)
               + lax.dot_general(slo, hi, TDOT, preferred_element_type=F32))
        )

    def tile(j):
        return gpart.at[
            pl.ds(pl.multiple_of((z % 4) * 32 + (j // 4) * 8, 8), 8), pl.ds(pl.multiple_of((j % 4) * 128, 128), 128)]

    def g_copy(k):
        peer = (m + k) % NM
        return pltpu.make_async_remote_copy(
            src_ref=tile(peer // 2), dst_ref=grecv.at[m],
            send_sem=g_send.at[k], recv_sem=g_recv.at[k], device_id=member(peer), device_id_type=MESH,
        )

    @pl.loop(1, NM)
    def _(k):
        g_copy(k).start()

    own_g = pltpu.make_async_copy(tile(chip), grecv.at[m], local_sem.at[2])
    own_g.start()

    wpart[...] = jnp.zeros_like(wpart)

    @pl.loop(0, COLS // CHUNK)
    def _(i):
        rows = pl.ds(pl.multiple_of(i * CHUNK, CHUNK), CHUNK)
        y = yall[rows, :]
        hi = y.astype(BF16)
        lo = (y - hi.astype(F32)).astype(BF16)
        b = recv_b[:, rows]
        wpart[...] += jnp.dot(b, hi, preferred_element_type=F32) + jnp.dot(b, lo, preferred_element_type=F32)

    own_g.wait()

    @pl.loop(1, NM)
    def _(k):
        g_copy(k).wait()

    gz[z] = jnp.sum(grecv[...], axis=0)

    def gz_copy(k):
        return pltpu.make_async_remote_copy(
            src_ref=gz.at[z], dst_ref=gz.at[z], send_sem=gz_send.at[k], recv_sem=gz_recv.at[k],
            device_id=at_z((z + k) % NZ), device_id_type=MESH,
        )

    def gz_arrived(k):
        piece = gz.at[mod(z - k, NZ)]
        pltpu.make_async_remote_copy(
            src_ref=piece, dst_ref=piece, send_sem=gz_send.at[k], recv_sem=gz_recv.at[k],
            device_id=at_z((z + k) % NZ), device_id_type=MESH,
        ).wait_recv()

    @pl.loop(1, NZ)
    def _(k):
        gz_copy(k).start()

    def w_copy(k):
        peer = (m + k) % NM
        return pltpu.make_async_remote_copy(
            src_ref=wpart.at[pl.ds(pl.multiple_of(peer * WIDE, WIDE), WIDE)], dst_ref=wrecv.at[m],
            send_sem=w_send.at[k], recv_sem=w_recv.at[k], device_id=member(peer), device_id_type=MESH,
        )

    own_w = pltpu.make_async_copy(
        wpart.at[pl.ds(pl.multiple_of(m * WIDE, WIDE), WIDE)], wrecv.at[m], local_sem.at[3])

    @pl.loop(1, NZ)
    def _(k):
        gz_arrived(k)

    def gp_copy(k):
        peer = (chip + k) % (NM // 2)
        return pltpu.make_async_remote_copy(
            src_ref=gz, dst_ref=gall_out.at[chip], send_sem=gp_send.at[k], recv_sem=gp_recv.at[k],
            device_id=member(peer * 2 + core), device_id_type=MESH,
        )

    @pl.loop(1, NM // 2)
    def _(k):
        gp_copy(k).start()

    own_w.start()

    @pl.loop(1, NM)
    def _(k):
        w_copy(k).start()

    gall_out[chip] = gz[...]
    own_w.wait()

    @pl.loop(1, NM)
    def _(k):
        w_copy(k).wait()

    rhs_out[pl.ds(BLK, WIDE), :] = jnp.sum(wrecv[...], axis=0)

    @pl.loop(1, NM // 2)
    def _(k):
        gp_copy(k).wait()

    @pl.loop(1, NZ)
    def _(k):
        gz_copy(k).wait_send()

    for chain in chains:
        first = chain[3]
        _, way, h, _ = chain
        buf = rup if way == 1 else rdn

        @pl.loop(first, 8)
        def _(s):
            rs_copy(chain, s, buf.at[s, :, halves[h]]).wait_send()

        @pl.loop(0, 8 - first)
        def _(s):
            ag_copy(chain, s).wait_send()


def exchange(packed, s_piece):
    vmem = pl.BlockSpec(memory_space=pltpu.VMEM)
    dma = pltpu.SemaphoreType.DMA
    return pl.pallas_call(
        comm_kernel,
        out_shape=(
            jax.ShapeDtypeStruct((NM // 2, NZ, 8, 128), F32),
            jax.ShapeDtypeStruct((BLK + WIDE, RANK), F32),
        ),
        in_specs=[vmem, vmem],
        out_specs=(vmem, vmem),
        scratch_shapes=[
            pltpu.VMEM((PW, COLS), BF16),
            pltpu.VMEM((NX, NT, WIDE, RANK), BF16),
            pltpu.VMEM((COLS, RANK), F32),
            pltpu.VMEM((COLS, RANK), F32),
            pltpu.VMEM((8, BLK, RANK), F32),
            pltpu.VMEM((8, BLK, RANK), F32),
            pltpu.VMEM((PW, RANK), F32),
            pltpu.VMEM((NM, WIDE, RANK), F32),
            pltpu.VMEM((128, RANK), F32),
            pltpu.VMEM((NM, 8, 128), F32),
            pltpu.VMEM((NZ, 8, 128), F32),
            dma((4,)),
            dma((NM,)), dma((NM,)),
            dma((NT,)), dma((NT,)),
            dma((4, 8)), dma((4, 8)),
            dma((4, 8)), dma((4, 8)),
            dma((NM,)), dma((NM,)),
            dma((NM,)), dma((NM,)),
            dma((NZ,)), dma((NZ,)),
            dma((NM // 2,)), dma((NM // 2,)),
        ],
        compiler_params=pltpu.CompilerParams(
            collective_id=0, has_side_effects=True, vmem_limit_bytes=48 * 1024 * 1024),
    )(packed, s_piece)


def shards(grad_buckets, sketch):
    z = lax.axis_index("dp") // NX
    packed = grad_buckets.reshape(WIDE, NZ, NM, BLK).transpose(2, 0, 1, 3).reshape(NM, WIDE, COLS)
    s_piece = lax.dynamic_slice_in_dim(sketch, z * (NX * WIDE), NX * WIDE, 0).reshape(NX, WIDE, RANK)
    gall, rhs = exchange(packed, s_piece)
    gram = gall.reshape(4, 4, NZ, 8, 128).transpose(2, 0, 3, 1, 4).reshape(RANK, RANK)
    lower = jnp.linalg.cholesky(gram)
    solved = jax.scipy.linalg.solve_triangular(lower, rhs.T, lower=True)
    basis_out = (solved[:, :BLK] * math.sqrt(ROWS)).astype(BF16)
    mine = solved[:, BLK:].astype(BF16).reshape(NZ * NX, RANK // (NZ * NX), WIDE)
    got = lax.all_to_all(mine, "dp", split_axis=0, concat_axis=0, tiled=True)
    projected = got.transpose(1, 0, 2).reshape(RANK // (NZ * NX), NZ * NX * WIDE)
    return basis_out, projected


def solution(mesh):
    in_specs = (P(("tensor", "dp"), None), P("tensor", None))
    out_specs = (P(None, ("dp", "tensor")), P("dp", "tensor"))
    return jax.shard_map(shards, mesh=mesh, in_specs=in_specs, out_specs=out_specs, check_vma=False)
```

time: 1510 us -> 363 us (0.24)
  waiting for transfers between devices: 1220 us -> 17.2 us
  Pallas kernels: 0 us -> 180 us
  blocking collectives: 107 us -> 0 us
    reduce_scatter x2 -> x0, waiting for transfers between devices: 724 us -> none  [the longest x1 695 us: shards(): projected = lax.psum_scatter(folded, 'dp', scatter_dimension=0, tiled=True)]
    psum x1 -> x0, waiting for transfers between devices: 471 us -> none  [shards(): gram_matrix = lax.psum(gram_of(sketch_piece), ('dp', 'tensor'))]
    pallas_call x0 -> x1, Pallas kernels: none -> 180 us  [exchange(): pl.pallas_call(comm_kernel, out_shape=(jax.ShapeDtypeStruct((NM // 2, NZ,...]
    all_to_all x1 -> x0, blocking collectives: 107 us -> none  [shards(): lax.all_to_all(split_view, 'dp', split_axis=1, concat_axis=0, tiled=True)]
    all_gather x1 -> x0, waiting for transfers between devices: 29 us -> none  [shards(): lax.all_gather(basis_piece, 'tensor', axis=1, tiled=True)]
    all_to_all x0 -> x1, waiting for transfers between devices: none -> 17.2 us  [shards(): got = lax.all_to_all(mine, 'dp', split_axis=0, concat_axis=0, tiled=True)]
  transfers between devices with their start and end apart: 4 -> 1, of which waited for: 4 -> 1; matrix products, arithmetic and copies ran while one was open for 0% -> 0% of each run, Pallas kernels for 0% -> 0%
where the time goes in v1:
time: 363 us; the launch traced here: 362 us
  Pallas kernels  180 us (50%)
  other arithmetic  119 us (33%)
  local copies, waits for them, and re-layouts  24.9 us (7%)
  waiting for transfers between devices  17.2 us (5%)
  starting transfers between devices  9.52 us (3%)
  matrix products  7.76 us (2%)
    pallas_call x1, Pallas kernels, exchange(): pl.pallas_call(comm_kernel, out_shape=(jax.ShapeDtypeStruct((NM // 2, NZ,...  180 us
    another operation x14, other arithmetic, shards(): lower = jnp.linalg.cholesky(gram)  78.8 us
    another operation x4, other arithmetic, shards(): solved = jax.scipy.linalg.solve_triangular(lower, rhs.T, lower=True)  40.3 us
    all_to_all x1, waiting for transfers between devices, shards(): got = lax.all_to_all(mine, 'dp', split_axis=0, concat_axis=0, tiled=True)  17.2 us
    another operation x12, local copies, waits for them, and re-layouts  10.9 us
    reshape x3, local copies, waits for them, and re-layouts, shards(): grad_buckets.reshape(WIDE, NZ, NM, BLK).transpose(2, 0, 1, 3)  10.1 us
    all_to_all x1, starting transfers between devices, shards(): got = lax.all_to_all(mine, 'dp', split_axis=0, concat_axis=0, tiled=True)  9.52 us
  transfers between devices with their start and end apart: 1, of which 1 were waited for; matrix products, arithmetic and copies ran while one was open for 0% of the time, Pallas kernels for 0%

profile of v1, /device:TPU:24, one launch (start us, length us, event | category | flops | bytes accessed | tf_op | source)
XLA Modules:
  0.0 362.3 jit_solution(2501187955115396805)
XLA Ops:
  0.7 4.1 %reshape.64 = bf16[16,16,32,112]{3,2,1,0:T(8,128)(2,1)S(1)} reshape(bf16[16,57344]{1,0:T(8,128)(2,1)} %param.2) | data formatting | bytes 3670016 | tf_op jit(solution)/shard_map/reshape | solution.py:359
  4.8 2.2 copy.26
  6.9 3.8 %reshape.65.packed = bf16[32,16,1792]{2,1,0:T(8,128)(2,1)S(1)} reshape(bf16[32,16,16,112]{3,2,1,0:T(8,128)(2,1)} %bitcast.70) | data formatting | bytes 3670016 | tf_op jit(solution)/shard_map/reshape | solution.py:359
  10.8 180.2 %shard_map.41 = (f32[16,16,8,128]{3,2,1,0:T(8,128)S(1)}, f32[128,512]{1,0:T(8,128)S(1)}) custom-call(bf16[32,16,1792]{2,1,0:T(8,128)(2,1)S(1)} %reshape.65.packed, bf16[4,16,512]{2,1,0:T(8,128)(2,1)S(1)} %bitcast.67), custom_call_target="tpu_custom_call" | custom-call | tf_op jit(solution)/shard_map/pallas_call | solution.py:322
  191.7 1.0 copy-done.1
  192.7 11.7 %cholesky.104 = f32[128,128]{1,0:T(8,128)S(1)} custom-call(f32[128,128]{1,0:T(8,128)S(1)} %cholesky.266), custom_call_target="Cholesky" | custom-call | tf_op jit(solution)/shard_map/jit(cholesky)/cholesky | solution.py:363
  204.6 9.8 %custom-call.31 = f32[1,128,128]{1,2,0:T(8,128)S(1)} custom-call(f32[1,128,128]{2,1,0:T(8,128)S(1)} %get-tuple-element.39), custom_call_target="InvertDiagBlocksLowerTriangular" | custom-call | tf_op jit(solution)/shard_map/jit(cholesky)/cholesky | solution.py:363
  214.4 1.2 constant_dynamic-update-slice_fusion.3
  215.7 1.3 convolution_subtract_fusion
  216.9 11.7 %cholesky.217 = f32[128,128]{1,0:T(8,128)S(1)} custom-call(f32[128,128]{1,0:T(8,128)S(1)} %cholesky.270), custom_call_target="Cholesky" | custom-call | tf_op jit(solution)/shard_map/jit(cholesky)/cholesky | solution.py:363
  228.7 9.9 %custom-call.32 = f32[1,128,128]{1,2,0:T(8,128)S(1)} custom-call(f32[1,128,128]{2,1,0:T(8,128)S(1)} %get-tuple-element.36), custom_call_target="InvertDiagBlocksLowerTriangular" | custom-call | tf_op jit(solution)/shard_map/jit(cholesky)/cholesky | solution.py:363
  238.9 1.3 convolution_subtract_fusion.1
  240.2 11.7 %cholesky.238 = f32[128,128]{1,0:T(8,128)S(1)} custom-call(f32[128,128]{1,0:T(8,128)S(1)} %cholesky.275), custom_call_target="Cholesky" | custom-call | tf_op jit(solution)/shard_map/jit(cholesky)/cholesky | solution.py:363
  251.9 9.8 %custom-call.33 = f32[1,128,128]{1,2,0:T(8,128)S(1)} custom-call(f32[1,128,128]{2,1,0:T(8,128)S(1)} %get-tuple-element.33), custom_call_target="InvertDiagBlocksLowerTriangular" | custom-call | tf_op jit(solution)/shard_map/jit(cholesky)/cholesky | solution.py:363
  262.0 1.2 convolution_subtract_fusion.5
  263.2 11.9 %cholesky.255 = f32[128,128]{1,0:T(8,128)S(1)} custom-call(f32[128,128]{1,0:T(8,128)S(1)} %convolution_subtract_fusion.5), custom_call_target="Cholesky" | custom-call | tf_op jit(solution)/shard_map/jit(cholesky)/cholesky | solution.py:363
  279.8 10.9 %while.1 = (s32[]{:T(128)}, f32[512,512]{1,0:T(8,128)S(1)}, s32[4,2]{0,1:T(2,128)S(1)}, f32[4,128,128]{2,1,0:T(8,128)}, s32[]{:T(128)}) while((s32[]{:T(128)}, f32[512,512]{1,0:T(8,128)S(1)}, s32[4,2]{0,1:T(2,128)S(1)}, f32[4,128,128]{2,1,0:T(8,128)}, s32[]{:T(128)}) %tuple.34), condition=%wide.while_cond, body=%wide.while_body.sunk | while | flops 2 | bytes 132205 | solution.py:364
  280.5 2.0 bitcast_dynamic-update-slice_fusion.2
  283.2 2.0 bitcast_dynamic-update-slice_fusion.2
  286.0 2.0 bitcast_dynamic-update-slice_fusion.2
  288.7 2.1 bitcast_dynamic-update-slice_fusion.2
  290.7 40.1 %custom-call.34 = f32[4,128,128]{1,2,0:T(8,128)S(1)} custom-call(f32[4,128,128]{2,1,0:T(8,128)} %get-tuple-element.13), custom_call_target="InvertDiagBlocksLowerTriangular" | custom-call | tf_op jit(solution)/shard_map/jit(_solve_triangular)/triangular_solve | solution.py:364
  334.0 9.5 %all-to-all-start = ((bf16[64,8,16]{2,1,0:T(8,128)(2,1)}), bf16[64,8,16]{2,1,0:T(8,128)(2,1)S(1)}, u32[]{:S(2)}, u32[]{:S(2)}) async-start(bf16[64,8,16]{2,1,0:T(8,128)(2,1)} %fusion.12), calls=%async_computation | async-start | bytes 262144 | tf_op jit(solution)/shard_map/all_to_all | solution.py:367
  344.3 17.2 %all-to-all-done = bf16[64,8,16]{2,1,0:T(8,128)(2,1)S(1)} async-done(((bf16[64,8,16]{2,1,0:T(8,128)(2,1)}), bf16[64,8,16]{2,1,0:T(8,128)(2,1)S(1)}, u32[]{:S(2)}, u32[]{:S(2)}) %all-to-all-start) | async-done | bytes 16416 | tf_op jit(solution)/shard_map/all_to_all | solution.py:367
  (45 shorter events, 10.9 us)
Async XLA Ops:
  0.6 10.2 %copy-start = (bf16[1024,512]{1,0:T(8,128)(2,1)S(1)}, bf16[1024,512]{1,0:T(8,128)(2,1)}, u32[]{:S(2)}) copy-start(bf16[1024,512]{1,0:T(8,128)(2,1)} %param.3) | copy-start | bytes 3145732
  191.7 1.0 copy-start.1
  334.0 27.5 %all-to-all-start = ((bf16[64,8,16]{2,1,0:T(8,128)(2,1)}), bf16[64,8,16]{2,1,0:T(8,128)(2,1)S(1)}, u32[]{:S(2)}, u32[]{:S(2)}) async-start(bf16[64,8,16]{2,1,0:T(8,128)(2,1)} %fusion.12), calls=%async_computation | async-start | bytes 262144 | tf_op jit(solution)/shard_map/all_to_all | solution.py:367

commit v2 on v1

--- a/solution.py
+++ b/solution.py
@@ -20,6 +20,11 @@
 PW = WIDE * NM
 HALF = RANK // 2
 CHUNK = 256
+N_DP = NZ * NX
+PER_DP = RANK // N_DP
+NB = 128
+GROUP = 8
+HIGHEST = lax.Precision.HIGHEST
 TDOT = (((0,), (0,)), ((), ()))
 
 
@@ -354,19 +359,134 @@
     )(packed, s_piece)
 
 
+def invert_factor(work):
+    for s in range(0, NB, GROUP):
+        n = NB - s
+        row = lax.broadcasted_iota(jnp.int32, (GROUP, NB), 0)
+        lane = lax.broadcasted_iota(jnp.int32, (GROUP, NB), 1)
+        rest = work[s:, :]
+        cols = [jnp.broadcast_to(rest[:, s + k : s + k + 1], (n, NB)) for k in range(GROUP)]
+        top = jnp.where((lane >= s) & (lane < s + GROUP), jnp.where(lane - s == row, 1.0, 0.0), rest[:GROUP])
+        below = rest[GROUP:]
+        if n > GROUP:
+            lane_b = lax.broadcasted_iota(jnp.int32, (n - GROUP, NB), 1)
+            below = jnp.where((lane_b >= s) & (lane_b < s + GROUP), 0.0, below)
+        for k in range(GROUP):
+            r = lax.rsqrt(jnp.broadcast_to(cols[k][k : k + 1], (GROUP, NB)))
+            mult = cols[k] * jnp.broadcast_to(r[:1], (n, NB))
+            for q in range(k + 1, GROUP):
+                cols[q] = cols[q] - mult * jnp.broadcast_to(mult[q : q + 1], (n, NB))
+            u = jnp.broadcast_to(top[k : k + 1], (GROUP, NB)) * r
+            top = jnp.where(row == k, u, jnp.where(row > k, top - mult[:GROUP] * u, top))
+            if n > GROUP:
+                below = below - mult[GROUP:] * jnp.broadcast_to(u[:1], (n - GROUP, NB))
+        work[s : s + GROUP, :] = top
+        if n > GROUP:
+            work[s + GROUP :, :] = below
+
+
+def finish_kernel(gall, rhs, basis_out, proj_out, mat, work, solved, outbox, inbox, sends, recvs):
+    dp = lax.axis_index("dp")
+    t = lax.axis_index("tensor")
+
+    barrier = pltpu.get_barrier_semaphore()
+
+    @pl.loop(1, N_DP)
+    def _(k):
+        pl.semaphore_signal(barrier, inc=1, device_id=((dp + k) % N_DP, t), device_id_type=MESH)
+
+    @pl.loop(0, NZ)
+    def _(z):
+        for j in range(NM // 2):
+            mat[pl.ds(pl.multiple_of(z * 32 + (j // 4) * 8, 8), 8), pl.ds((j % 4) * 128, 128)] = gall[j, z]
+
+    mat[:, RANK:] = rhs[...].T
+
+    @pl.loop(0, RANK // NB)
+    def _(j):
+        rows = pl.ds(pl.multiple_of(j * NB, NB), NB)
+        work[...] = mat[rows, rows]
+        invert_factor(work)
+        row = lax.broadcasted_iota(jnp.int32, (NB, NB), 0)
+        lane = lax.broadcasted_iota(jnp.int32, (NB, NB), 1)
+        inverse = jnp.where(lane <= row, work[...], 0.0)
+        upper = jnp.dot(inverse, mat[rows, :], precision=HIGHEST, preferred_element_type=F32)
+        solved[rows, :] = upper[:, RANK:]
+        for i in range(1, RANK // NB):
+            @pl.when(i > j)
+            def _():
+                mat[i * NB : (i + 1) * NB, :] -= lax.dot_general(
+                    upper[:, i * NB : (i + 1) * NB], upper, TDOT, precision=HIGHEST, preferred_element_type=F32)
+
+    packed = jnp.zeros((N_DP, NB), F32)
+    lane = lax.broadcasted_iota(jnp.int32, (N_DP, NB), 1)
+    for r in range(PER_DP):
+        part = solved[pl.ds(r, N_DP, stride=PER_DP), :]
+        slot = PER_DP - 1 - r
+        packed = jnp.where(lane // WIDE == slot, pltpu.roll(part, (WIDE * slot - BLK) % NB, 1), packed)
+    outbox[...] = packed.reshape(N_DP, 1, NB)
+
+    pl.semaphore_wait(barrier, N_DP - 1)
+
+    def copy(k):
+        peer = (dp + k) % N_DP
+        return pltpu.make_async_remote_copy(
+            src_ref=outbox.at[peer], dst_ref=inbox.at[dp], send_sem=sends.at[k], recv_sem=recvs.at[k],
+            device_id=(peer, t), device_id_type=MESH,
+        )
+
+    @pl.loop(1, N_DP)
+    def _(k):
+        copy(k).start()
+
+    inbox[dp] = outbox[dp]
+    basis_out[...] = (solved[:, :BLK] * math.sqrt(ROWS)).astype(BF16)
+
+    @pl.loop(1, N_DP)
+    def _(k):
+        copy(k).wait()
+
+    per_tile = NB // WIDE
+    lane = lax.broadcasted_iota(jnp.int32, (PER_DP, NB), 1)
+    for q in range(N_DP // per_tile):
+        tile = jnp.zeros((PER_DP, NB), F32)
+        for i in range(per_tile):
+            line = jnp.broadcast_to(inbox[q * per_tile + i], (PER_DP, NB))
+            line = pltpu.roll(line, 0, 1, stride=WIDE, stride_axis=0)
+            line = pltpu.roll(line, (WIDE * (i + 1)) % NB, 1)
+            tile = jnp.where(lane // WIDE == i, line, tile)
+        proj_out[:, q * NB : (q + 1) * NB] = tile.astype(BF16)
+
+
+def finish(gall, rhs):
+    vmem = pl.BlockSpec(memory_space=pltpu.VMEM)
+    return pl.pallas_call(
+        finish_kernel,
+        out_shape=(
+            jax.ShapeDtypeStruct((RANK, BLK), BF16),
+            jax.ShapeDtypeStruct((PER_DP, N_DP * WIDE), BF16),
+        ),
+        in_specs=[vmem, vmem],
+        out_specs=(vmem, vmem),
+        scratch_shapes=[
+            pltpu.VMEM((RANK, RANK + NB), F32),
+            pltpu.VMEM((NB, NB), F32),
+            pltpu.VMEM((RANK, NB), F32),
+            pltpu.VMEM((N_DP, 1, NB), F32),
+            pltpu.VMEM((N_DP, 1, NB), F32),
+            pltpu.SemaphoreType.DMA((N_DP,)),
+            pltpu.SemaphoreType.DMA((N_DP,)),
+        ],
+        compiler_params=pltpu.CompilerParams(
+            collective_id=1, has_side_effects=True, vmem_limit_bytes=32 * 1024 * 1024),
+    )(gall, rhs)
+
+
 def shards(grad_buckets, sketch):
     z = lax.axis_index("dp") // NX
     packed = grad_buckets.reshape(WIDE, NZ, NM, BLK).transpose(2, 0, 1, 3).reshape(NM, WIDE, COLS)
     s_piece = lax.dynamic_slice_in_dim(sketch, z * (NX * WIDE), NX * WIDE, 0).reshape(NX, WIDE, RANK)
-    gall, rhs = exchange(packed, s_piece)
-    gram = gall.reshape(4, 4, NZ, 8, 128).transpose(2, 0, 3, 1, 4).reshape(RANK, RANK)
-    lower = jnp.linalg.cholesky(gram)
-    solved = jax.scipy.linalg.solve_triangular(lower, rhs.T, lower=True)
-    basis_out = (solved[:, :BLK] * math.sqrt(ROWS)).astype(BF16)
-    mine = solved[:, BLK:].astype(BF16).reshape(NZ * NX, RANK // (NZ * NX), WIDE)
-    got = lax.all_to_all(mine, "dp", split_axis=0, concat_axis=0, tiled=True)
-    projected = got.transpose(1, 0, 2).reshape(RANK // (NZ * NX), NZ * NX * WIDE)
-    return basis_out, projected
+    return finish(*exchange(packed, s_piece))
 
 
 def solution(mesh):

time: 363 us -> 229 us (0.63)
  other arithmetic: 119 us -> 0 us
  Pallas kernels: 180 us -> 213 us
  waiting for transfers between devices: 17.2 us -> 0 us
  local copies, waits for them, and re-layouts: 24.9 us -> 14 us
  starting transfers between devices: 9.52 us -> 0 us
  matrix products: 7.76 us -> 0 us
    another operation x18 -> x0, other arithmetic: 119 us -> none  [the longest x14 78.8 us: shards(): lower = jnp.linalg.cholesky(gram)]
    pallas_call x0 -> x1, Pallas kernels: none -> 33.4 us  [finish(): pl.pallas_call(finish_kernel, out_shape=(jax.ShapeDtypeStruct((RANK, BLK)...]
    all_to_all x1 -> x0, waiting for transfers between devices: 17.2 us -> none  [shards(): got = lax.all_to_all(mine, 'dp', split_axis=0, concat_axis=0, tiled=True)]
    another operation x17 -> x0, local copies, waits for them, and re-layouts: 11 us -> none
    all_to_all x1 -> x0, starting transfers between devices: 9.52 us -> none  [shards(): got = lax.all_to_all(mine, 'dp', split_axis=0, concat_axis=0, tiled=True)]
    another operation x13 -> x0, matrix products: 7.76 us -> none  [the longest x6 5.46 us: shards(): lower = jnp.linalg.cholesky(gram)]
  transfers between devices with their start and end apart: 1 -> 0, of which waited for: 1 -> 0; matrix products, arithmetic and copies ran while one was open for 0% -> 0% of each run, Pallas kernels for 0% -> 0%
where the time goes in v2:
time: 229 us; the launch traced here: 228 us
  Pallas kernels  213 us (93%)
  local copies, waits for them, and re-layouts  14 us (6%)
    pallas_call x1, Pallas kernels, exchange(): pl.pallas_call(comm_kernel, out_shape=(jax.ShapeDtypeStruct((NM // 2, NZ,...  180 us
    pallas_call x1, Pallas kernels, finish(): pl.pallas_call(finish_kernel, out_shape=(jax.ShapeDtypeStruct((RANK, BLK)...  33.4 us
    reshape x3, local copies, waits for them, and re-layouts, shards(): grad_buckets.reshape(WIDE, NZ, NM, BLK).transpose(2, 0, 1, 3)  12.7 us

profile of v2, /device:TPU:24, one launch (start us, length us, event | category | flops | bytes accessed | tf_op | source)
XLA Modules:
  0.0 228.1 jit_solution(900834062198013958)
XLA Ops:
  0.6 0.0 copy-start
  0.6 5.1 %reshape.13 = bf16[16,16,32,112]{3,2,1,0:T(8,128)(2,1)} reshape(bf16[16,57344]{1,0:T(8,128)(2,1)} %param.2) | data formatting | bytes 3670016 | tf_op jit(solution)/shard_map/reshape | solution.py:487
  5.8 3.7 %copy.7 = bf16[16,16,32,112]{3,1,0,2:T(8,128)(2,1)} copy(bf16[16,16,32,112]{3,2,1,0:T(8,128)(2,1)} %reshape.13) | data formatting | bytes 3670016 | tf_op jit(solution)/shard_map/reshape | solution.py:487
  9.5 3.8 %reshape.14.packed = bf16[32,16,1792]{2,1,0:T(8,128)(2,1)S(1)} reshape(bf16[32,16,16,112]{3,2,1,0:T(8,128)(2,1)} %bitcast.7) | data formatting | bytes 3670016 | tf_op jit(solution)/shard_map/reshape | solution.py:487
  13.3 0.0 copy-done
  13.4 180.0 %shard_map.41 = (f32[16,16,8,128]{3,2,1,0:T(8,128)S(1)}, f32[128,512]{1,0:T(8,128)S(1)}) custom-call(bf16[32,16,1792]{2,1,0:T(8,128)(2,1)S(1)} %reshape.14.packed, bf16[4,16,512]{2,1,0:T(8,128)(2,1)S(1)} %bitcast.6), custom_call_target="tpu_custom_call" | custom-call | tf_op jit(solution)/shard_map/pallas_call | solution.py:327
  193.3 33.4 %shard_map.42 = (bf16[512,112]{1,0:T(8,128)(2,1)S(1)}, bf16[8,1024]{1,0:T(8,128)(2,1)S(1)}) custom-call(f32[16,16,8,128]{3,2,1,0:T(8,128)S(1)} %get-tuple-element.4.gall, f32[128,512]{1,0:T(8,128)S(1)} %get-tuple-element.5.rhs), custom_call_target="tpu_custom_call" | custom-call | tf_op jit(solution)/shard_map/pallas_call | solution.py:463
  226.7 0.8 copy.5
  227.4 0.6 copy.9
  (1 shorter events, 0.0 us)
Async XLA Ops:
  0.6 12.7 %copy-start = (bf16[1024,512]{1,0:T(8,128)(2,1)S(1)}, bf16[1024,512]{1,0:T(8,128)(2,1)}, u32[]{:S(2)}) copy-start(bf16[1024,512]{1,0:T(8,128)(2,1)} %param.3) | copy-start | bytes 3145732

commit v3 on v2

--- a/solution.py
+++ b/solution.py
@@ -19,7 +19,7 @@
 COLS = BLK * NZ
 PW = WIDE * NM
 HALF = RANK // 2
-CHUNK = 256
+PARTS = (0, 384, 896, 1280, 1792)
 N_DP = NZ * NX
 PER_DP = RANK // N_DP
 NB = 128
@@ -32,11 +32,26 @@
     return lax.rem(a + n, n)
 
 
+def near(k):
+    if k == 0:
+        return NZ - 1
+    if abs(k) == NZ // 2:
+        return 0
+    return NZ - 1 - 2 * k if k > 0 else NZ + 2 * k
+
+
+ORDER = sorted(range(1 - NZ // 2, NZ // 2 + 1), key=near)
+
+
+def await_bytes(ref, sem):
+    pltpu.make_async_copy(ref, ref, sem).wait()
+
+
 def comm_kernel(
-    packed, s_piece, gall_out, rhs_out,
-    recv_b, recv_s, ypart, yall, rup, rdn, wpart, wrecv, gpart, grecv, gz,
+    grad, sketch, gall_out, rhs_out,
+    packed, recv_b, recv_s, ypart, yall, rup, rdn, wpart, wsib, wrecv, gpart, grecv, gz,
     local_sem, a2a_send, a2a_recv, s_send, s_recv, rs_send, rs_recv, ag_send, ag_recv,
-    g_send, g_recv, w_send, w_recv, gz_send, gz_recv, gp_send, gp_recv,
+    g_send, g_recv, pair_send, pair_recv, w_send, w_recv, gz_send, gz_recv, gp_send, gp_recv, gs_send, gs_recv,
 ):
     dp = lax.axis_index("dp")
     t = lax.axis_index("tensor")
@@ -53,6 +68,7 @@
         return (i * NX + x, t)
 
     zup, zdn = at_z(mod(z + 1, NZ)), at_z(mod(z - 1, NZ))
+    sibling = (dp, t + 1 - 2 * core)
 
     barrier = pltpu.get_barrier_semaphore()
 
@@ -64,35 +80,49 @@
     def _(k):
         pl.semaphore_signal(barrier, inc=1, device_id=at_z((z + k) % NZ), device_id_type=MESH)
 
-    pl.semaphore_wait(barrier, NM - 1 + NZ - 1)
-
-    def b_copy(k):
+    mine = pl.ds(pl.multiple_of(m * WIDE, WIDE), WIDE)
+
+    def pack(c):
+        @pl.loop(0, NM // 8)
+        def _(q):
+            for place in range(4 * c, 4 * c + 4):
+                first = ((z + ORDER[place] + NZ) % NZ) * (NM * BLK) + q * (8 * BLK)
+                part = grad[:, pl.ds(pl.multiple_of(first, 128), 8 * BLK)]
+                for i in range(8):
+                    packed[q * 8 + i, :, place * BLK : (place + 1) * BLK] = part[:, i * BLK : (i + 1) * BLK]
+
+    def b_copy(c, k):
         peer = (m + k) % NM
-        return pltpu.make_async_remote_copy(
-            src_ref=packed.at[peer], dst_ref=recv_b.at[pl.ds(pl.multiple_of(m * WIDE, WIDE), WIDE)],
-            send_sem=a2a_send.at[k], recv_sem=a2a_recv.at[k], device_id=member(peer), device_id_type=MESH,
+        lanes = pl.ds(PARTS[c], PARTS[c + 1] - PARTS[c])
+        return pltpu.make_async_remote_copy(
+            src_ref=packed.at[peer, :, lanes], dst_ref=recv_b.at[mine, lanes],
+            send_sem=a2a_send.at[c], recv_sem=a2a_recv.at[c], device_id=member(peer), device_id_type=MESH,
         )
 
     def s_copy(k):
         peer = (t + k) % NT
         return pltpu.make_async_remote_copy(
-            src_ref=s_piece, dst_ref=recv_s.at[:, t],
+            src_ref=sketch.at[z], dst_ref=recv_s.at[:, t],
             send_sem=s_send.at[k], recv_sem=s_recv.at[k], device_id=(dp, peer), device_id_type=MESH,
         )
 
-    @pl.loop(1, NT)
-    def _(k):
-        s_copy(k).start()
-
-    @pl.loop(1, NM)
-    def _(k):
-        b_copy(k).start()
-
-    own_b = pltpu.make_async_copy(
-        packed.at[m], recv_b.at[pl.ds(pl.multiple_of(m * WIDE, WIDE), WIDE)], local_sem.at[0])
-    own_s = pltpu.make_async_copy(s_piece, recv_s.at[:, t], local_sem.at[1])
+    own_s = pltpu.make_async_copy(sketch.at[z], recv_s.at[:, t], local_sem.at[0])
+    own_s.start()
+    for c in range(4):
+        pack(c)
+        if c == 0:
+            pl.semaphore_wait(barrier, NM - 1 + NZ - 1)
+
+            @pl.loop(1, NT)
+            def _(k):
+                s_copy(k).start()
+
+        @pl.loop(1, NM)
+        def _(k):
+            b_copy(c, k).start()
+
+    own_b = pltpu.make_async_copy(packed.at[m], recv_b.at[mine], local_sem.at[1])
     own_b.start()
-    own_s.start()
     own_b.wait()
     own_s.wait()
 
@@ -100,18 +130,8 @@
     def _(k):
         s_copy(k).wait()
 
-    @pl.loop(1, NM)
-    def _(k):
-        b_copy(k).wait()
-
-    @pl.loop(0, COLS // CHUNK)
-    def _(i):
-        rows = pl.ds(pl.multiple_of(i * CHUNK, CHUNK), CHUNK)
-        ypart[rows, :] = lax.dot_general(
-            recv_b[:, rows], recv_s[...].reshape(PW, RANK), TDOT, preferred_element_type=F32)
-
-    def block(b):
-        return pl.ds(pl.multiple_of(mod(b, NZ) * BLK, 8), BLK)
+    def rows_of(k):
+        return pl.ds(near(k) * BLK, BLK)
 
     halves = (pl.ds(0, HALF), pl.ds(HALF, HALF))
     chains = ((0, 1, 0, 0), (1, -1, 1, 0), (2, 1, 1, 1), (3, -1, 0, 1))
@@ -125,29 +145,28 @@
             device_id=zup if way == 1 else zdn, device_id_type=MESH,
         )
 
-    def rs_first(chain):
-        _, way, h, s = chain
-        rs_copy(chain, s, ypart.at[block(z + way * (8 - s)), halves[h]]).start()
-
-    def rs_next(chain, s):
-        _, way, h, _ = chain
-        buf = rup if way == 1 else rdn
-        slot = buf.at[s - 1, :, halves[h]]
-        rs_copy(chain, s - 1, slot).wait_recv()
-        buf[s - 1, :, halves[h]] += ypart[block(z + way * (8 - s)), halves[h]]
-        rs_copy(chain, s, slot).start()
-
-    for chain in chains:
-        rs_first(chain)
-    for chain in chains[:2]:
-        rs_next(chain, 1)
-
-    @pl.loop(2, 8)
-    def _(s):
+    def rs_step(s):
         for chain in chains:
-            rs_next(chain, s)
-
-    own = block(z)
+            _, way, h, first = chain
+            rows = rows_of(way * (8 - s))
+            if s == first:
+                rs_copy(chain, s, ypart.at[rows, halves[h]]).start()
+            elif s > first:
+                buf = rup if way == 1 else rdn
+                slot = buf.at[s - 1, :, halves[h]]
+                rs_copy(chain, s - 1, slot).wait_recv()
+                buf[s - 1, :, halves[h]] += ypart[rows, halves[h]]
+                rs_copy(chain, s, slot).start()
+
+    for c in range(4):
+        lanes = pl.ds(PARTS[c], PARTS[c + 1] - PARTS[c])
+        await_bytes(recv_b.at[pl.ds(0, (NM - 1) * WIDE), lanes], a2a_recv.at[c])
+        ypart[lanes, :] = lax.dot_general(
+            recv_b[:, lanes], recv_s[...].reshape(PW, RANK), TDOT, preferred_element_type=F32)
+        rs_step(2 * c)
+        rs_step(2 * c + 1)
+
+    own = rows_of(0)
     for chain in chains:
         _, way, h, _ = chain
         rs_copy(chain, 7, (rup if way == 1 else rdn).at[7, :, halves[h]]).wait_recv()
@@ -155,55 +174,50 @@
 
     def ag_copy(chain, s):
         name, way, h, _ = chain
-        piece = yall.at[block(z - way * s), halves[h]]
-        return pltpu.make_async_remote_copy(
-            src_ref=piece, dst_ref=piece, send_sem=ag_send.at[name, s], recv_sem=ag_recv.at[name, s],
+        return pltpu.make_async_remote_copy(
+            src_ref=yall.at[rows_of(-way * s), halves[h]], dst_ref=yall.at[rows_of(-way * (s + 1)), halves[h]],
+            send_sem=ag_send.at[name, s], recv_sem=ag_recv.at[name, s],
             device_id=zup if way == 1 else zdn, device_id_type=MESH,
         )
 
-    def ag_arrived(chain, s):
-        name, way, h, _ = chain
-        piece = yall.at[block(z - way * (s + 1)), halves[h]]
-        pltpu.make_async_remote_copy(
-            src_ref=piece, dst_ref=piece, send_sem=ag_send.at[name, s], recv_sem=ag_recv.at[name, s],
-            device_id=zup if way == 1 else zdn, device_id_type=MESH,
-        ).wait_recv()
-
-    for chain in chains:
-        ag_copy(chain, 0).start()
-    rhs_out[pl.ds(0, BLK), :] = yall[own, :]
-
-    @pl.loop(1, 7)
-    def _(s):
-        for chain in chains:
-            ag_arrived(chain, s - 1)
-            ag_copy(chain, s).start()
-
-    for chain in chains[:2]:
-        ag_arrived(chain, 6)
-        ag_copy(chain, 7).start()
-    for chain in chains[2:]:
-        ag_arrived(chain, 6)
-    for chain in chains[:2]:
-        ag_arrived(chain, 7)
-
     gcols = pl.ds(pl.multiple_of((z // 4) * 128, 128), 128)
-    gpart[...] = jnp.zeros_like(gpart)
-
-    @pl.loop(0, COLS // CHUNK)
-    def _(i):
-        rows = pl.ds(pl.multiple_of(i * CHUNK, CHUNK), CHUNK)
+
+    def use(c):
+        rows = pl.ds(PARTS[c], PARTS[c + 1] - PARTS[c])
         y = yall[rows, :]
         hi = y.astype(BF16)
         lo = (y - hi.astype(F32)).astype(BF16)
         ys = yall[rows, gcols]
         shi = ys.astype(BF16)
         slo = (ys - shi.astype(F32)).astype(BF16)
-        gpart[...] += (
+        b = recv_b[:, rows]
+        g = (
             lax.dot_general(shi, hi, TDOT, preferred_element_type=F32)
             + (lax.dot_general(shi, lo, TDOT, preferred_element_type=F32)
                + lax.dot_general(slo, hi, TDOT, preferred_element_type=F32))
         )
+        w = jnp.dot(b, hi, preferred_element_type=F32) + jnp.dot(b, lo, preferred_element_type=F32)
+        w = w.reshape(NM // 2, 2, WIDE, RANK)
+        if c == 3:
+            gpart[...] = g
+            wpart[...] = w
+        else:
+            gpart[...] += g
+            wpart[...] += w
+
+    for s in range(8):
+        for chain in chains:
+            if s < 8 - chain[3]:
+                if s:
+                    ag_copy(chain, s - 1).wait_recv()
+                ag_copy(chain, s).start()
+        if s == 0:
+            rhs_out[pl.ds(0, BLK), :] = yall[own, :]
+        if s in (2, 4, 6):
+            use(4 - s // 2)
+    for chain in chains:
+        ag_copy(chain, 7 - chain[3]).wait_recv()
+    use(0)
 
     def tile(j):
         return gpart.at[
@@ -220,20 +234,12 @@
     def _(k):
         g_copy(k).start()
 
+    pair = pltpu.make_async_remote_copy(
+        src_ref=wpart.at[:, 1 - core], dst_ref=wsib, send_sem=pair_send, recv_sem=pair_recv,
+        device_id=sibling, device_id_type=MESH)
+    pair.start()
     own_g = pltpu.make_async_copy(tile(chip), grecv.at[m], local_sem.at[2])
     own_g.start()
-
-    wpart[...] = jnp.zeros_like(wpart)
-
-    @pl.loop(0, COLS // CHUNK)
-    def _(i):
-        rows = pl.ds(pl.multiple_of(i * CHUNK, CHUNK), CHUNK)
-        y = yall[rows, :]
-        hi = y.astype(BF16)
-        lo = (y - hi.astype(F32)).astype(BF16)
-        b = recv_b[:, rows]
-        wpart[...] += jnp.dot(b, hi, preferred_element_type=F32) + jnp.dot(b, lo, preferred_element_type=F32)
-
     own_g.wait()
 
     @pl.loop(1, NM)
@@ -259,24 +265,27 @@
     def _(k):
         gz_copy(k).start()
 
+    pair.wait()
+    wsib[...] += wpart[:, core]
+
     def w_copy(k):
-        peer = (m + k) % NM
-        return pltpu.make_async_remote_copy(
-            src_ref=wpart.at[pl.ds(pl.multiple_of(peer * WIDE, WIDE), WIDE)], dst_ref=wrecv.at[m],
-            send_sem=w_send.at[k], recv_sem=w_recv.at[k], device_id=member(peer), device_id_type=MESH,
-        )
-
-    own_w = pltpu.make_async_copy(
-        wpart.at[pl.ds(pl.multiple_of(m * WIDE, WIDE), WIDE)], wrecv.at[m], local_sem.at[3])
+        peer = (chip + k) % (NM // 2)
+        return pltpu.make_async_remote_copy(
+            src_ref=wsib.at[peer], dst_ref=wrecv.at[chip],
+            send_sem=w_send.at[k], recv_sem=w_recv.at[k], device_id=member(peer * 2 + core), device_id_type=MESH,
+        )
 
     @pl.loop(1, NZ)
     def _(k):
         gz_arrived(k)
+
+    half = pl.ds(core * (NZ // 2), NZ // 2)
 
     def gp_copy(k):
         peer = (chip + k) % (NM // 2)
         return pltpu.make_async_remote_copy(
-            src_ref=gz, dst_ref=gall_out.at[chip], send_sem=gp_send.at[k], recv_sem=gp_recv.at[k],
+            src_ref=gz.at[half], dst_ref=gall_out.at[chip, half],
+            send_sem=gp_send.at[k], recv_sem=gp_recv.at[k],
             device_id=member(peer * 2 + core), device_id_type=MESH,
         )
 
@@ -284,16 +293,37 @@
     def _(k):
         gp_copy(k).start()
 
-    own_w.start()
-
-    @pl.loop(1, NM)
+    @pl.loop(1, NM // 2)
     def _(k):
         w_copy(k).start()
 
     gall_out[chip] = gz[...]
-    own_w.wait()
-
-    @pl.loop(1, NM)
+    wrecv[chip] = wsib[chip]
+
+    def gs_copy(k):
+        piece = gall_out.at[mod(chip - k, NM // 2), half]
+        return pltpu.make_async_remote_copy(
+            src_ref=piece, dst_ref=piece, send_sem=gs_send.at[k], recv_sem=gs_recv.at[k],
+            device_id=sibling, device_id_type=MESH,
+        )
+
+    def gs_arrived(k):
+        piece = gall_out.at[mod(chip - k, NM // 2), pl.ds((1 - core) * (NZ // 2), NZ // 2)]
+        pltpu.make_async_remote_copy(
+            src_ref=piece, dst_ref=piece, send_sem=gs_send.at[k], recv_sem=gs_recv.at[k],
+            device_id=sibling, device_id_type=MESH,
+        ).wait_recv()
+
+    @pl.loop(1, NM // 2)
+    def _(k):
+        gp_copy(k).wait()
+        gs_copy(k).start()
+
+    @pl.loop(1, NM // 2)
+    def _(k):
+        gs_arrived(k)
+
+    @pl.loop(1, NM // 2)
     def _(k):
         w_copy(k).wait()
 
@@ -301,27 +331,23 @@
 
     @pl.loop(1, NM // 2)
     def _(k):
-        gp_copy(k).wait()
+        gs_copy(k).wait_send()
 
     @pl.loop(1, NZ)
     def _(k):
         gz_copy(k).wait_send()
 
+    for c in range(4):
+        await_bytes(recv_b.at[pl.ds(0, (NM - 1) * WIDE), pl.ds(PARTS[c], PARTS[c + 1] - PARTS[c])], a2a_send.at[c])
     for chain in chains:
-        first = chain[3]
-        _, way, h, _ = chain
-        buf = rup if way == 1 else rdn
-
-        @pl.loop(first, 8)
-        def _(s):
-            rs_copy(chain, s, buf.at[s, :, halves[h]]).wait_send()
-
-        @pl.loop(0, 8 - first)
-        def _(s):
+        _, way, h, first = chain
+        for s in range(first, 8):
+            rs_copy(chain, s, (rup if way == 1 else rdn).at[s, :, halves[h]]).wait_send()
+        for s in range(0, 8 - first):
             ag_copy(chain, s).wait_send()
 
 
-def exchange(packed, s_piece):
+def exchange(grad_buckets, sketch):
     vmem = pl.BlockSpec(memory_space=pltpu.VMEM)
     dma = pltpu.SemaphoreType.DMA
     return pl.pallas_call(
@@ -330,33 +356,37 @@
             jax.ShapeDtypeStruct((NM // 2, NZ, 8, 128), F32),
             jax.ShapeDtypeStruct((BLK + WIDE, RANK), F32),
         ),
-        in_specs=[vmem, vmem],
+        in_specs=[vmem, pl.BlockSpec(memory_space=pl.ANY)],
         out_specs=(vmem, vmem),
         scratch_shapes=[
+            pltpu.VMEM((NM, WIDE, COLS), BF16),
             pltpu.VMEM((PW, COLS), BF16),
             pltpu.VMEM((NX, NT, WIDE, RANK), BF16),
             pltpu.VMEM((COLS, RANK), F32),
             pltpu.VMEM((COLS, RANK), F32),
             pltpu.VMEM((8, BLK, RANK), F32),
             pltpu.VMEM((8, BLK, RANK), F32),
-            pltpu.VMEM((PW, RANK), F32),
-            pltpu.VMEM((NM, WIDE, RANK), F32),
+            pltpu.VMEM((NM // 2, 2, WIDE, RANK), F32),
+            pltpu.VMEM((NM // 2, WIDE, RANK), F32),
+            pltpu.VMEM((NM // 2, WIDE, RANK), F32),
             pltpu.VMEM((128, RANK), F32),
             pltpu.VMEM((NM, 8, 128), F32),
             pltpu.VMEM((NZ, 8, 128), F32),
-            dma((4,)),
-            dma((NM,)), dma((NM,)),
+            dma((3,)),
+            dma((4,)), dma((4,)),
             dma((NT,)), dma((NT,)),
             dma((4, 8)), dma((4, 8)),
             dma((4, 8)), dma((4, 8)),
             dma((NM,)), dma((NM,)),
-            dma((NM,)), dma((NM,)),
+            dma, dma,
+            dma((NM // 2,)), dma((NM // 2,)),
             dma((NZ,)), dma((NZ,)),
+            dma((NM // 2,)), dma((NM // 2,)),
             dma((NM // 2,)), dma((NM // 2,)),
         ],
         compiler_params=pltpu.CompilerParams(
             collective_id=0, has_side_effects=True, vmem_limit_bytes=48 * 1024 * 1024),
-    )(packed, s_piece)
+    )(grad_buckets, sketch)
 
 
 def invert_factor(work):
@@ -483,10 +513,7 @@
 
 
 def shards(grad_buckets, sketch):
-    z = lax.axis_index("dp") // NX
-    packed = grad_buckets.reshape(WIDE, NZ, NM, BLK).transpose(2, 0, 1, 3).reshape(NM, WIDE, COLS)
-    s_piece = lax.dynamic_slice_in_dim(sketch, z * (NX * WIDE), NX * WIDE, 0).reshape(NX, WIDE, RANK)
-    return finish(*exchange(packed, s_piece))
+    return finish(*exchange(grad_buckets, sketch.reshape(NZ, NX, WIDE, RANK)))
 
 
 def solution(mesh):

time: 229 us -> 194 us (0.85)
  Pallas kernels: 213 us -> 188 us
  local copies, waits for them, and re-layouts: 14 us -> 4.08 us
    pallas_call x1, Pallas kernels: 180 us -> 155 us  [exchange(): pl.pallas_call(comm_kernel, out_shape=(jax.ShapeDtypeStruct((NM // 2, NZ,...]
    reshape x3 -> x0, local copies, waits for them, and re-layouts: 12.7 us -> none  [shards(): grad_buckets.reshape(WIDE, NZ, NM, BLK).transpose(2, 0, 1, 3)]
    unnamed x3 -> x5, local copies, waits for them, and re-layouts: 0.61 us -> 3.32 us
where the time goes in v3:
time: 194 us; the launch traced here: 193 us
  Pallas kernels  188 us (97%)
  local copies, waits for them, and re-layouts  4.08 us (2%)
    pallas_call x1, Pallas kernels, exchange(): pl.pallas_call(comm_kernel, out_shape=(jax.ShapeDtypeStruct((NM // 2, NZ,...  155 us
    pallas_call x1, Pallas kernels, finish(): pl.pallas_call(finish_kernel, out_shape=(jax.ShapeDtypeStruct((RANK, BLK)...  33.3 us

profile of v3, /device:TPU:24, one launch (start us, length us, event | category | flops | bytes accessed | tf_op | source)
XLA Modules:
  0.0 192.7 jit_solution(4118359235787549257)
XLA Ops:
  0.6 0.0 copy-start
  0.6 1.5 copy-done
  2.1 0.0 copy-start.1
  2.1 1.2 copy-done.1
  3.4 154.7 %shard_map.41 = (f32[16,16,8,128]{3,2,1,0:T(8,128)S(1)}, f32[128,512]{1,0:T(8,128)S(1)}) custom-call(bf16[16,57344]{1,0:T(8,128)(2,1)S(1)} %copy-done, bf16[16,4,16,512]{3,2,1,0:T(8,128)(2,1)S(1)} %bitcast.1), custom_call_target="tpu_custom_call" | custom-call | tf_op jit(solution)/shard_map/pallas_call | solution.py:353
  158.0 33.3 %shard_map.42 = (bf16[512,112]{1,0:T(8,128)(2,1)S(1)}, bf16[8,1024]{1,0:T(8,128)(2,1)S(1)}) custom-call(f32[16,16,8,128]{3,2,1,0:T(8,128)S(1)} %get-tuple-element.4.gall, f32[128,512]{1,0:T(8,128)S(1)} %get-tuple-element.5.rhs), custom_call_target="tpu_custom_call" | custom-call | tf_op jit(solution)/shard_map/pallas_call | solution.py:493
  191.3 0.8 copy.4
  192.1 0.6 copy.6
Async XLA Ops:
  0.6 1.5 copy-start
  2.1 1.2 copy-start.1

commit v4 on v0

v4 whole, which is shorter than its diff:
```python
import math

import jax
import jax.numpy as jnp
from jax import lax
from jax.experimental import pallas as pl
from jax.experimental.pallas import tpu as pltpu
from jax.sharding import PartitionSpec as P

MESH = pl.DeviceIdType.MESH
F32 = jnp.float32
BF16 = jnp.bfloat16
NZ, NX, NT = 16, 4, 8
NM = NX * NT
NCHIP = NM // 2
ROWS = 57344
RANK = 512
WIDE = 16
BLK = ROWS // (NZ * NM)
COLS = BLK * NZ
PW = WIDE * NM
HALF = RANK // 2
PARTS = (0, 384, 896, 1280, 1792)
N_DP = NZ * NX
PER_DP = RANK // N_DP
NB = 128
GROUP = 8
HIGHEST = lax.Precision.HIGHEST
TDOT = (((0,), (0,)), ((), ()))


def mod(a, n):
    return lax.rem(a + n, n)


def near(k):
    if k == 0:
        return NZ - 1
    if abs(k) == NZ // 2:
        return 0
    return NZ - 1 - 2 * k if k > 0 else NZ + 2 * k


ORDER = sorted(range(1 - NZ // 2, NZ // 2 + 1), key=near)


def await_bytes(ref, sem):
    pltpu.make_async_copy(ref, ref, sem).wait()


def invert_factor(work):
    for s in range(0, NB, GROUP):
        n = NB - s
        row = lax.broadcasted_iota(jnp.int32, (GROUP, NB), 0)
        lane = lax.broadcasted_iota(jnp.int32, (GROUP, NB), 1)
        rest = work[s:, :]
        cols = [jnp.broadcast_to(rest[:, s + k : s + k + 1], (n, NB)) for k in range(GROUP)]
        top = jnp.where((lane >= s) & (lane < s + GROUP), jnp.where(lane - s == row, 1.0, 0.0), rest[:GROUP])
        below = rest[GROUP:]
        if n > GROUP:
            lane_b = lax.broadcasted_iota(jnp.int32, (n - GROUP, NB), 1)
            below = jnp.where((lane_b >= s) & (lane_b < s + GROUP), 0.0, below)
        for k in range(GROUP):
            r = lax.rsqrt(jnp.broadcast_to(cols[k][k : k + 1], (GROUP, NB)))
            mult = cols[k] * jnp.broadcast_to(r[:1], (n, NB))
            for q in range(k + 1, GROUP):
                cols[q] = cols[q] - mult * jnp.broadcast_to(mult[q : q + 1], (n, NB))
            u = jnp.broadcast_to(top[k : k + 1], (GROUP, NB)) * r
            top = jnp.where(row == k, u, jnp.where(row > k, top - mult[:GROUP] * u, top))
            if n > GROUP:
                below = below - mult[GROUP:] * jnp.broadcast_to(u[:1], (n - GROUP, NB))
        work[s : s + GROUP, :] = top
        if n > GROUP:
            work[s + GROUP :, :] = below


def kernel(
    grad, sketch, basis_out, proj_out,
    packed, recv_b, recv_s, ypart, yall, rup, rdn, wpart, wsib, wrecv,
    gown, gsib, grecv, gzs, gzr, gza, gall, rhs, mat, work, inverses, solved, outbox, inbox_x, inbox_z,
    local_sem, a2a_send, a2a_recv, s_send, s_recv, rs_send, rs_recv, ag_send, ag_recv,
    pair_send, pair_recv, w_send, w_recv, g_send, g_recv, gzs_send, gzs_recv, gza_send, gza_recv,
    gp_send, gp_recv, gs_send, gs_recv, x_send, x_recv, z_send, z_recv,
):
    dp = lax.axis_index("dp")
    t = lax.axis_index("tensor")
    z = dp // NX
    x = dp % NX
    m = x * NT + t
    chip = m // 2
    core = m % 2

    def member(i):
        return (z * NX + i // NT, i % NT)

    def at_z(i):
        return (i * NX + x, t)

    zup, zdn = at_z(mod(z + 1, NZ)), at_z(mod(z - 1, NZ))
    sibling = (dp, t + 1 - 2 * core)

    barrier = pltpu.get_barrier_semaphore()

    @pl.loop(1, NM)
    def _(k):
        pl.semaphore_signal(barrier, inc=1, device_id=member((m + k) % NM), device_id_type=MESH)

    @pl.loop(1, NZ)
    def _(k):
        pl.semaphore_signal(barrier, inc=1, device_id=at_z((z + k) % NZ), device_id_type=MESH)

    mine = pl.ds(pl.multiple_of(m * WIDE, WIDE), WIDE)

    def pack(c):
        @pl.loop(0, NM // 8)
        def _(q):
            for place in range(4 * c, 4 * c + 4):
                first = ((z + ORDER[place] + NZ) % NZ) * (NM * BLK) + q * (8 * BLK)
                part = grad[:, pl.ds(pl.multiple_of(first, 128), 8 * BLK)]
                for i in range(8):
                    packed[q * 8 + i, :, place * BLK : (place + 1) * BLK] = part[:, i * BLK : (i + 1) * BLK]

    def b_copy(c, k):
        peer = (m + k) % NM
        lanes = pl.ds(PARTS[c], PARTS[c + 1] - PARTS[c])
        return pltpu.make_async_remote_copy(
            src_ref=packed.at[peer, :, lanes], dst_ref=recv_b.at[mine, lanes],
            send_sem=a2a_send.at[c], recv_sem=a2a_recv.at[c], device_id=member(peer), device_id_type=MESH,
        )

    def s_copy(k):
        peer = (t + k) % NT
        return pltpu.make_async_remote_copy(
            src_ref=sketch.at[z], dst_ref=recv_s.at[:, t],
            send_sem=s_send.at[k], recv_sem=s_recv.at[k], device_id=(dp, peer), device_id_type=MESH,
        )

    own_s = pltpu.make_async_copy(sketch.at[z], recv_s.at[:, t], local_sem.at[0])
    own_s.start()

    def send(c):
        @pl.loop(1, NM)
        def _(k):
            b_copy(c, k).start()

    pack(0)
    pl.semaphore_wait(barrier, NM - 1 + NZ - 1)

    @pl.loop(1, NT)
    def _(k):
        s_copy(k).start()

    send(0)
    pack(1)
    send(1)
    pack(2)
    pack(3)

    own_b = pltpu.make_async_copy(packed.at[m], recv_b.at[mine], local_sem.at[1])
    own_b.start()
    own_b.wait()
    own_s.wait()

    @pl.loop(1, NT)
    def _(k):
        s_copy(k).wait()

    def rows_of(k):
        return pl.ds(near(k) * BLK, BLK)

    halves = (pl.ds(0, HALF), pl.ds(HALF, HALF))
    chains = ((0, 1, 0, 0), (1, -1, 1, 0), (2, 1, 1, 1), (3, -1, 0, 1))

    def rs_copy(chain, s, src):
        name, way, h, _ = chain
        buf = rup if way == 1 else rdn
        return pltpu.make_async_remote_copy(
            src_ref=src, dst_ref=buf.at[s, :, halves[h]],
            send_sem=rs_send.at[name, s], recv_sem=rs_recv.at[name, s],
            device_id=zup if way == 1 else zdn, device_id_type=MESH,
        )

    def rs_step(s):
        for chain in chains:
            _, way, h, first = chain
            rows = rows_of(way * (8 - s))
            if s == first:
                rs_copy(chain, s, ypart.at[rows, halves[h]]).start()
            elif s > first:
                buf = rup if way == 1 else rdn
                slot = buf.at[s - 1, :, halves[h]]
                rs_copy(chain, s - 1, slot).wait_recv()
                buf[s - 1, :, halves[h]] += ypart[rows, halves[h]]
                rs_copy(chain, s, slot).start()

    for c in range(4):
        lanes = pl.ds(PARTS[c], PARTS[c + 1] - PARTS[c])
        await_bytes(recv_b.at[pl.ds(0, (NM - 1) * WIDE), lanes], a2a_recv.at[c])
        ypart[lanes, :] = lax.dot_general(
            recv_b[:, lanes], recv_s[...].reshape(PW, RANK), TDOT, preferred_element_type=F32)
        rs_step(2 * c)
        if c < 2:
            send(c + 2)
        rs_step(2 * c + 1)

    own = rows_of(0)
    for chain in chains:
        _, way, h, _ = chain
        rs_copy(chain, 7, (rup if way == 1 else rdn).at[7, :, halves[h]]).wait_recv()
    yall[own, :] = ypart[own, :] + rup[7] + rdn[7]

    def ag_copy(chain, s):
        name, way, h, _ = chain
        return pltpu.make_async_remote_copy(
            src_ref=yall.at[rows_of(-way * s), halves[h]], dst_ref=yall.at[rows_of(-way * (s + 1)), halves[h]],
            send_sem=ag_send.at[name, s], recv_sem=ag_recv.at[name, s],
            device_id=zup if way == 1 else zdn, device_id_type=MESH,
        )

    def use(c):
        rows = pl.ds(PARTS[c], PARTS[c + 1] - PARTS[c])
        y = yall[rows, :]
        hi = y.astype(BF16)
        lo = (y - hi.astype(F32)).astype(BF16)
        b = recv_b[:, rows]
        w = jnp.dot(b, hi, preferred_element_type=F32) + jnp.dot(b, lo, preferred_element_type=F32)
        w = w.reshape(NCHIP, 2, WIDE, RANK)
        if c == 3:
            wpart[...] = w
        else:
            wpart[...] += w

    def to_sibling(src, dst, send_sem, recv_sem):
        return pltpu.make_async_remote_copy(
            src_ref=src, dst_ref=dst, send_sem=send_sem, recv_sem=recv_sem, device_id=sibling, device_id_type=MESH)

    g_pair = to_sibling(gown.at[1 - core], gsib, pair_send.at[0], pair_recv.at[0])
    w_pair = to_sibling(wpart.at[:, 1 - core], wsib, pair_send.at[1], pair_recv.at[1])

    def plane_copy(k, src, dst, send_sem, recv_sem):
        return pltpu.make_async_remote_copy(
            src_ref=src, dst_ref=dst, send_sem=send_sem, recv_sem=recv_sem,
            device_id=member(((chip + k) % NCHIP) * 2 + core), device_id_type=MESH)

    def z_copy(k, src, dst, send_sem, recv_sem):
        return pltpu.make_async_remote_copy(
            src_ref=src, dst_ref=dst, send_sem=send_sem, recv_sem=recv_sem,
            device_id=at_z((z + k) % NZ), device_id_type=MESH)

    def gram_1():
        y = yall[own, :]
        rhs[pl.ds(0, BLK), :] = y
        rhs[pl.ds(BLK, WIDE), :] = jnp.zeros((WIDE, RANK), F32)
        gram = lax.dot_general(y, y, TDOT, precision=HIGHEST, preferred_element_type=F32)
        gown[...] = gram.reshape(2, NCHIP, NZ, RANK)
        g_pair.start()

    def gram_2():
        g_pair.wait()
        gsib[...] += gown[core]

        @pl.loop(1, NCHIP)
        def _(k):
            plane_copy(k, gsib.at[(chip + k) % NCHIP], grecv.at[chip], g_send, g_recv).start()

        grecv[chip] = gsib[chip]

    def gram_3():
        await_bytes(grecv.at[pl.ds(0, NCHIP - 1)], g_recv)
        gzs[...] = jnp.sum(grecv[...], axis=0).reshape(NZ, 1, RANK)

        @pl.loop(1, NZ)
        def _(k):
            z_copy(k, gzs.at[(z + k) % NZ], gzr.at[z], gzs_send, gzs_recv).start()

        gzr[z] = gzs[z]

    def gram_4():
        await_bytes(gzr.at[pl.ds(0, NZ - 1)], gzs_recv)
        gza[z] = jnp.sum(gzr[...], axis=0)

        @pl.loop(1, NZ)
        def _(k):
            z_copy(k, gza.at[z], gza.at[z], gza_send, gza_recv).start()

    def gp_copy(k):
        piece = gall.at[core, chip]
        return plane_copy(k, piece, piece, gp_send.at[k], gp_recv.at[k])

    def gs_copy(k):
        piece = gall.at[core, mod(chip - k, NCHIP)]
        return to_sibling(piece, piece, gs_send.at[k], gs_recv.at[k])

    def gram_5():
        await_bytes(gza.at[pl.ds(0, NZ - 1)], gza_recv)
        gall[core, chip] = gza[...].reshape(NZ, RANK)

        @pl.loop(1, NCHIP)
        def _(k):
            gp_copy(k).start()

        gs_copy(0).start()

    def gram_6():
        @pl.loop(1, NCHIP)
        def _(k):
            piece = gall.at[core, mod(chip - k, NCHIP)]
            plane_copy(k, piece, piece, gp_send.at[k], gp_recv.at[k]).wait_recv()
            gs_copy(k).start()

    def gram_7():
        @pl.loop(0, NCHIP)
        def _(k):
            piece = gall.at[1 - core, mod(chip - k, NCHIP)]
            to_sibling(piece, piece, gs_send.at[k], gs_recv.at[k]).wait_recv()

    beside = (gram_1, gram_2, lambda: use(3), gram_3, gram_4, lambda: use(2), gram_5, lambda: use(1))

    for s in range(8):
        for chain in chains:
            if s < 8 - chain[3]:
                if s:
                    ag_copy(chain, s - 1).wait_recv()
                ag_copy(chain, s).start()
        beside[s]()
    for chain in chains:
        ag_copy(chain, 7 - chain[3]).wait_recv()
    use(0)
    w_pair.start()
    gram_6()
    gram_7()

    def w_send_off():
        w_pair.wait()
        wsib[...] += wpart[:, core]

        @pl.loop(1, NCHIP)
        def _(k):
            plane_copy(k, wsib.at[(chip + k) % NCHIP], wrecv.at[chip], w_send, w_recv).start()

        wrecv[chip] = wsib[chip]

    def below(i):
        return pl.ds(i * NB, NB)

    def w_catch_up(steps):
        await_bytes(wrecv.at[pl.ds(0, NCHIP - 1)], w_recv)
        w = jnp.concatenate([jnp.zeros((BLK, RANK), F32), jnp.sum(wrecv[...], axis=0)], axis=0).T
        for j in range(steps):
            part = jnp.dot(inverses[j], w[:NB], precision=HIGHEST, preferred_element_type=F32)
            solved[below(j), :] += part
            w = w[NB:] - lax.dot_general(
                mat[below(j), (j + 1) * NB : RANK], part, TDOT, precision=HIGHEST, preferred_element_type=F32)
        mat[steps * NB :, RANK:] += w

    mat[:, :RANK] = gall[...].reshape(RANK, RANK)
    mat[:, RANK:] = rhs[...].T

    @pl.loop(0, RANK // NB)
    def _(j):
        rows = pl.ds(pl.multiple_of(j * NB, NB), NB)
        work[...] = mat[rows, rows]
        invert_factor(work)

        @pl.when(j == 0)
        def _():
            w_send_off()

        @pl.when(j == 2)
        def _():
            w_catch_up(2)

        row = lax.broadcasted_iota(jnp.int32, (NB, NB), 0)
        lane = lax.broadcasted_iota(jnp.int32, (NB, NB), 1)
        inverse = jnp.where(lane <= row, work[...], 0.0)
        inverses[j] = inverse
        upper = jnp.dot(inverse, mat[rows, :], precision=HIGHEST, preferred_element_type=F32)
        mat[rows, :] = upper
        solved[rows, :] = upper[:, RANK:]
        for i in range(1, RANK // NB):
            @pl.when(i > j)
            def _():
                mat[below(i), :] -= lax.dot_general(
                    upper[:, i * NB : (i + 1) * NB], upper, TDOT, precision=HIGHEST, preferred_element_type=F32)

    packed_p = jnp.zeros((N_DP, NB), F32)
    lane = lax.broadcasted_iota(jnp.int32, (N_DP, NB), 1)
    for r in range(PER_DP):
        part = solved[pl.ds(r, N_DP, stride=PER_DP), :]
        slot = PER_DP - 1 - r
        packed_p = jnp.where(lane // WIDE == slot, pltpu.roll(part, (WIDE * slot - BLK) % NB, 1), packed_p)
    outbox[...] = packed_p.reshape(NZ, NX, 1, NB)

    def x_copy(k):
        peer = (x + k) % NX
        return pltpu.make_async_remote_copy(
            src_ref=outbox.at[:, peer], dst_ref=inbox_x.at[x], send_sem=x_send.at[k], recv_sem=x_recv.at[k],
            device_id=(z * NX + peer, t), device_id_type=MESH,
        )

    for k in range(1, NX):
        x_copy(k).start()
    inbox_x[x] = outbox[:, x]
    basis_out[...] = (solved[:, :BLK] * math.sqrt(ROWS)).astype(BF16)
    for k in range(1, NX):
        x_copy(k).wait()

    @pl.loop(1, NZ)
    def _(k):
        z_copy(k, inbox_x.at[:, (z + k) % NZ], inbox_z.at[z], z_send, z_recv).start()

    inbox_z[z] = inbox_x[:, z]

    for ref, sem in (
        (grecv.at[pl.ds(0, NCHIP - 1)], g_send), (wrecv.at[pl.ds(0, NCHIP - 1)], w_send),
        (gzr.at[pl.ds(0, NZ - 1)], gzs_send), (gza.at[pl.ds(0, NZ - 1)], gza_send),
    ):
        await_bytes(ref, sem)

    @pl.loop(0, NCHIP)
    def _(k):
        gs_copy(k).wait_send()

    @pl.loop(1, NCHIP)
    def _(k):
        gp_copy(k).wait_send()

    for c in range(4):
        await_bytes(recv_b.at[pl.ds(0, (NM - 1) * WIDE), pl.ds(PARTS[c], PARTS[c + 1] - PARTS[c])], a2a_send.at[c])
    for chain in chains:
        _, way, h, first = chain
        for s in range(first, 8):
            rs_copy(chain, s, (rup if way == 1 else rdn).at[s, :, halves[h]]).wait_send()
        for s in range(0, 8 - first):
            ag_copy(chain, s).wait_send()

    await_bytes(inbox_z.at[pl.ds(0, NZ - 1)], z_send)
    await_bytes(inbox_z.at[pl.ds(0, NZ - 1)], z_recv)
    per_tile = NB // WIDE
    lane = lax.broadcasted_iota(jnp.int32, (PER_DP, NB), 1)
    for q in range(N_DP // per_tile):
        tile = jnp.zeros((PER_DP, NB), F32)
        for i in range(per_tile):
            src = q * per_tile + i
            line = jnp.broadcast_to(inbox_z[src // NX, src % NX], (PER_DP, NB))
            line = pltpu.roll(line, 0, 1, stride=WIDE, stride_axis=0)
            line = pltpu.roll(line, (WIDE * (i + 1)) % NB, 1)
            tile = jnp.where(lane // WIDE == i, line, tile)
        proj_out[:, q * NB : (q + 1) * NB] = tile.astype(BF16)


def project(grad_buckets, sketch):
    vmem = pl.BlockSpec(memory_space=pltpu.VMEM)
    dma = pltpu.SemaphoreType.DMA
    return pl.pallas_call(
        kernel,
        out_shape=(
            jax.ShapeDtypeStruct((RANK, BLK), BF16),
            jax.ShapeDtypeStruct((PER_DP, N_DP * WIDE), BF16),
        ),
        in_specs=[vmem, pl.BlockSpec(memory_space=pl.ANY)],
        out_specs=(vmem, vmem),
        scratch_shapes=[
            pltpu.VMEM((NM, WIDE, COLS), BF16),
            pltpu.VMEM((PW, COLS), BF16),
            pltpu.VMEM((NX, NT, WIDE, RANK), BF16),
            pltpu.VMEM((COLS, RANK), F32),
            pltpu.VMEM((COLS, RANK), F32),
            pltpu.VMEM((8, BLK, RANK), F32),
            pltpu.VMEM((8, BLK, RANK), F32),
            pltpu.VMEM((NCHIP, 2, WIDE, RANK), F32),
            pltpu.VMEM((NCHIP, WIDE, RANK), F32),
            pltpu.VMEM((NCHIP, WIDE, RANK), F32),
            pltpu.VMEM((2, NCHIP, NZ, RANK), F32),
            pltpu.VMEM((NCHIP, NZ, RANK), F32),
            pltpu.VMEM((NCHIP, NZ, RANK), F32),
            pltpu.VMEM((NZ, 1, RANK), F32),
            pltpu.VMEM((NZ, 1, RANK), F32),
            pltpu.VMEM((NZ, 1, RANK), F32),
            pltpu.VMEM((2, NCHIP, NZ, RANK), F32),
            pltpu.VMEM((BLK + WIDE, RANK), F32),
            pltpu.VMEM((RANK, RANK + NB), F32),
            pltpu.VMEM((NB, NB), F32),
            pltpu.VMEM((RANK // NB, NB, NB), F32),
            pltpu.VMEM((RANK, NB), F32),
            pltpu.VMEM((NZ, NX, 1, NB), F32),
            pltpu.VMEM((NX, NZ, 1, NB), F32),
            pltpu.VMEM((NZ, NX, 1, NB), F32),
            dma((2,)),
            dma((4,)), dma((4,)),
            dma((NT,)), dma((NT,)),
            dma((4, 8)), dma((4, 8)),
            dma((4, 8)), dma((4, 8)),
            dma((2,)), dma((2,)),
            dma, dma, dma, dma, dma, dma, dma, dma,
            dma((NCHIP,)), dma((NCHIP,)),
            dma((NCHIP,)), dma((NCHIP,)),
            dma((NX,)), dma((NX,)),
            dma, dma,
        ],
        compiler_params=pltpu.CompilerParams(
            collective_id=0, has_side_effects=True, vmem_limit_bytes=56 * 1024 * 1024),
    )(grad_buckets, sketch)


def shards(grad_buckets, sketch):
    return project(grad_buckets, sketch.reshape(NZ, NX, WIDE, RANK))


def solution(mesh):
    in_specs = (P(("tensor", "dp"), None), P("tensor", None))
    out_specs = (P(None, ("dp", "tensor")), P("dp", "tensor"))
    return jax.shard_map(shards, mesh=mesh, in_specs=in_specs, out_specs=out_specs, check_vma=False)
```

time: 1510 us -> 162 us (0.11)
  waiting for transfers between devices: 1220 us -> 0 us
  Pallas kernels: 0 us -> 155 us
  other arithmetic: 121 us -> 0 us
  blocking collectives: 107 us -> 0 us
  matrix products: 22 us -> 0 us
  between operations: 17 us -> 0.64 us
    reduce_scatter x2 -> x0, waiting for transfers between devices: 724 us -> none  [the longest x1 695 us: shards(): projected = lax.psum_scatter(folded, 'dp', scatter_dimension=0, tiled=True)]
    psum x1 -> x0, waiting for transfers between devices: 471 us -> none  [shards(): gram_matrix = lax.psum(gram_of(sketch_piece), ('dp', 'tensor'))]
    pallas_call x0 -> x1, Pallas kernels: none -> 155 us  [project(): pl.pallas_call(kernel, out_shape=(jax.ShapeDtypeStruct((RANK, BLK), BF16)...]
    another operation x18 -> x0, other arithmetic: 120 us -> none  [the longest x14 78.6 us: shards(): lower_factor = jnp.linalg.cholesky(gram_matrix)]
    all_to_all x1 -> x0, blocking collectives: 107 us -> none  [shards(): lax.all_to_all(split_view, 'dp', split_axis=1, concat_axis=0, tiled=True)]
    all_gather x1 -> x0, waiting for transfers between devices: 29 us -> none  [shards(): lax.all_gather(basis_piece, 'tensor', axis=1, tiled=True)]
  transfers between devices with their start and end apart: 4 -> 0, of which waited for: 4 -> 0; matrix products, arithmetic and copies ran while one was open for 0% -> 0% of each run, Pallas kernels for 0% -> 0%
where the time goes in v4:
time: 162 us; the launch traced here: 159 us
  Pallas kernels  155 us (96%)
  local copies, waits for them, and re-layouts  2.97 us (2%)
    pallas_call x1, Pallas kernels, project(): pl.pallas_call(kernel, out_shape=(jax.ShapeDtypeStruct((RANK, BLK), BF16)...  155 us

profile of v4, /device:TPU:24, one launch (start us, length us, event | category | flops | bytes accessed | tf_op | source)
XLA Modules:
  0.0 158.9 jit_solution(17420002929214027082)
XLA Ops:
  0.6 155.3 %shard_map.41 = (bf16[512,112]{1,0:T(8,128)(2,1)}, bf16[8,1024]{1,0:T(8,128)(2,1)}) custom-call(bf16[16,57344]{1,0:T(8,128)(2,1)} %grad.1, bf16[16,4,16,512]{3,2,1,0:T(8,128)(2,1)} %bitcast.1), custom_call_target="tpu_custom_call" | custom-call | tf_op jit(solution)/shard_map/pallas_call | solution.py:455
  155.9 1.7 %copy.4 = bf16[512,112]{0,1:T(8,128)(2,1)} copy(bf16[512,112]{1,0:T(8,128)(2,1)} %get-tuple-element.2) | data formatting | bytes 229376 | tf_op jit(solution)/shard_map/pallas_call | solution.py:455
  157.6 1.3 copy.6

commit v5 on v4

--- a/solution.py
+++ b/solution.py
@@ -20,7 +20,9 @@
 COLS = BLK * NZ
 PW = WIDE * NM
 HALF = RANK // 2
-PARTS = (0, 384, 896, 1280, 1792)
+PARTS = (0, 128, 384, 896, 1280, 1792)
+STEPS = ((0,), (1,), (2, 3), (4, 5), (6, 7))
+USES = (0, 384, 896, 1280, 1792)
 N_DP = NZ * NX
 PER_DP = RANK // N_DP
 NB = 128
@@ -48,8 +50,10 @@
     pltpu.make_async_copy(ref, ref, sem).wait()
 
 
-def invert_factor(work):
+def invert_factor(work, halfway):
     for s in range(0, NB, GROUP):
+        if s == NB // 2:
+            halfway()
         n = NB - s
         row = lax.broadcasted_iota(jnp.int32, (GROUP, NB), 0)
         lane = lax.broadcasted_iota(jnp.int32, (GROUP, NB), 1)
@@ -151,8 +155,8 @@
         s_copy(k).start()
 
     send(0)
+    send(1)
     pack(1)
-    send(1)
     pack(2)
     pack(3)
 
@@ -193,15 +197,15 @@
                 buf[s - 1, :, halves[h]] += ypart[rows, halves[h]]
                 rs_copy(chain, s, slot).start()
 
-    for c in range(4):
+    for c in range(len(STEPS)):
         lanes = pl.ds(PARTS[c], PARTS[c + 1] - PARTS[c])
         await_bytes(recv_b.at[pl.ds(0, (NM - 1) * WIDE), lanes], a2a_recv.at[c])
+        if 0 < c < len(STEPS) - 1:
+            send(c + 1)
         ypart[lanes, :] = lax.dot_general(
             recv_b[:, lanes], recv_s[...].reshape(PW, RANK), TDOT, preferred_element_type=F32)
-        rs_step(2 * c)
-        if c < 2:
-            send(c + 2)
-        rs_step(2 * c + 1)
+        for s in STEPS[c]:
+            rs_step(s)
 
     own = rows_of(0)
     for chain in chains:
@@ -218,7 +222,7 @@
         )
 
     def use(c):
-        rows = pl.ds(PARTS[c], PARTS[c + 1] - PARTS[c])
+        rows = pl.ds(USES[c], USES[c + 1] - USES[c])
         y = yall[rows, :]
         hi = y.astype(BF16)
         lo = (y - hi.astype(F32)).astype(BF16)
@@ -314,20 +318,33 @@
             piece = gall.at[1 - core, mod(chip - k, NCHIP)]
             to_sibling(piece, piece, gs_send.at[k], gs_recv.at[k]).wait_recv()
 
-    beside = (gram_1, gram_2, lambda: use(3), gram_3, gram_4, lambda: use(2), gram_5, lambda: use(1))
-
-    for s in range(8):
+    def gather_step(s):
         for chain in chains:
             if s < 8 - chain[3]:
                 if s:
                     ag_copy(chain, s - 1).wait_recv()
                 ag_copy(chain, s).start()
-        beside[s]()
-    for chain in chains:
-        ag_copy(chain, 7 - chain[3]).wait_recv()
-    use(0)
-    w_pair.start()
+
+    def gather_end():
+        for chain in chains:
+            ag_copy(chain, 7 - chain[3]).wait_recv()
+
+    gather_step(0)
+    gram_1()
+    gather_step(1)
+    gram_2()
+    gather_step(2)
+    gram_3()
+    gather_step(3)
+    gram_4()
+    use(3)
+    gather_step(4)
+    gram_5()
+    use(2)
+    gather_step(5)
     gram_6()
+    gather_step(6)
+    use(1)
     gram_7()
 
     def w_send_off():
@@ -343,15 +360,20 @@
     def below(i):
         return pl.ds(i * NB, NB)
 
-    def w_catch_up(steps):
+    def w_solve():
         await_bytes(wrecv.at[pl.ds(0, NCHIP - 1)], w_recv)
         w = jnp.concatenate([jnp.zeros((BLK, RANK), F32), jnp.sum(wrecv[...], axis=0)], axis=0).T
-        for j in range(steps):
+        for j in range(RANK // NB):
             part = jnp.dot(inverses[j], w[:NB], precision=HIGHEST, preferred_element_type=F32)
             solved[below(j), :] += part
-            w = w[NB:] - lax.dot_general(
-                mat[below(j), (j + 1) * NB : RANK], part, TDOT, precision=HIGHEST, preferred_element_type=F32)
-        mat[steps * NB :, RANK:] += w
+            if j + 1 < RANK // NB:
+                w = w[NB:] - lax.dot_general(
+                    mat[below(j), (j + 1) * NB : RANK], part, TDOT, precision=HIGHEST, preferred_element_type=F32)
+
+    def at(j, now, work_beside):
+        @pl.when(j == now)
+        def _():
+            work_beside()
 
     mat[:, :RANK] = gall[...].reshape(RANK, RANK)
     mat[:, RANK:] = rhs[...].T
@@ -360,16 +382,19 @@
     def _(j):
         rows = pl.ds(pl.multiple_of(j * NB, NB), NB)
         work[...] = mat[rows, rows]
-        invert_factor(work)
-
-        @pl.when(j == 0)
-        def _():
-            w_send_off()
-
-        @pl.when(j == 2)
-        def _():
-            w_catch_up(2)
-
+
+        def halfway():
+            at(j, 0, lambda: gather_step(7))
+            at(j, 2, w_send_off)
+
+        invert_factor(work, halfway)
+
+        def last_of_w():
+            gather_end()
+            use(0)
+            w_pair.start()
+
+        at(j, 1, last_of_w)
         row = lax.broadcasted_iota(jnp.int32, (NB, NB), 0)
         lane = lax.broadcasted_iota(jnp.int32, (NB, NB), 1)
         inverse = jnp.where(lane <= row, work[...], 0.0)
@@ -383,6 +408,8 @@
                 mat[below(i), :] -= lax.dot_general(
                     upper[:, i * NB : (i + 1) * NB], upper, TDOT, precision=HIGHEST, preferred_element_type=F32)
 
+    w_solve()
+
     packed_p = jnp.zeros((N_DP, NB), F32)
     lane = lax.broadcasted_iota(jnp.int32, (N_DP, NB), 1)
     for r in range(PER_DP):
@@ -425,7 +452,7 @@
     def _(k):
         gp_copy(k).wait_send()
 
-    for c in range(4):
+    for c in range(len(STEPS)):
         await_bytes(recv_b.at[pl.ds(0, (NM - 1) * WIDE), pl.ds(PARTS[c], PARTS[c + 1] - PARTS[c])], a2a_send.at[c])
     for chain in chains:
         _, way, h, first = chain
@@ -487,7 +514,7 @@
             pltpu.VMEM((NX, NZ, 1, NB), F32),
             pltpu.VMEM((NZ, NX, 1, NB), F32),
             dma((2,)),
-            dma((4,)), dma((4,)),
+            dma((len(STEPS),)), dma((len(STEPS),)),
             dma((NT,)), dma((NT,)),
             dma((4, 8)), dma((4, 8)),
             dma((4, 8)), dma((4, 8)),

time: 162 us -> 155 us (0.957); the launches traced: 159 us -> 155 us
  Pallas kernels: 155 us -> 151 us
    pallas_call x1, Pallas kernels: 155 us -> 151 us  [project(): pl.pallas_call(kernel, out_shape=(jax.ShapeDtypeStruct((RANK, BLK), BF16)...]
where the time goes in v5:
time: 155 us
  Pallas kernels  151 us (97%)
  local copies, waits for them, and re-layouts  2.97 us (2%)
    pallas_call x1, Pallas kernels, project(): pl.pallas_call(kernel, out_shape=(jax.ShapeDtypeStruct((RANK, BLK), BF16)...  151 us

profile of v5, /device:TPU:24, one launch (start us, length us, event | category | flops | bytes accessed | tf_op | source)
XLA Modules:
  0.0 155.1 jit_solution(12811610275935110876)
XLA Ops:
  0.6 151.5 %shard_map.41 = (bf16[512,112]{1,0:T(8,128)(2,1)}, bf16[8,1024]{1,0:T(8,128)(2,1)}) custom-call(bf16[16,57344]{1,0:T(8,128)(2,1)} %grad.1, bf16[16,4,16,512]{3,2,1,0:T(8,128)(2,1)} %bitcast.1), custom_call_target="tpu_custom_call" | custom-call | tf_op jit(solution)/shard_map/pallas_call | solution.py:482
  152.1 1.7 %copy.4 = bf16[512,112]{0,1:T(8,128)(2,1)} copy(bf16[512,112]{1,0:T(8,128)(2,1)} %get-tuple-element.2) | data formatting | bytes 229376 | tf_op jit(solution)/shard_map/pallas_call | solution.py:482
  153.8 1.3 copy.6

commit v6 on v5

--- a/solution.py
+++ b/solution.py
@@ -27,6 +27,7 @@
 PER_DP = RANK // N_DP
 NB = 128
 GROUP = 8
+GR, GL = 8, 640
 HIGHEST = lax.Precision.HIGHEST
 TDOT = (((0,), (0,)), ((), ()))
 
@@ -79,9 +80,9 @@
 
 
 def kernel(
-    grad, sketch, basis_out, proj_out,
-    packed, recv_b, recv_s, ypart, yall, rup, rdn, wpart, wsib, wrecv,
-    gown, gsib, grecv, gzs, gzr, gza, gall, rhs, mat, work, inverses, solved, outbox, inbox_x, inbox_z,
+    grad_hbm, sketch, basis_out, proj_out,
+    grad, packed, recv_b, recv_s, ypart, yall, rup, rdn, wpart, wsib, wrecv,
+    ysib, gown, grecv, gzs, gzr, gza, gall, rhs, mat, work, inverses, solved, outbox, inbox_x, inbox_z,
     local_sem, a2a_send, a2a_recv, s_send, s_recv, rs_send, rs_recv, ag_send, ag_recv,
     pair_send, pair_recv, w_send, w_recv, g_send, g_recv, gzs_send, gzs_recv, gza_send, gza_recv,
     gp_send, gp_recv, gs_send, gs_recv, x_send, x_recv, z_send, z_recv,
@@ -103,6 +104,9 @@
     zup, zdn = at_z(mod(z + 1, NZ)), at_z(mod(z - 1, NZ))
     sibling = (dp, t + 1 - 2 * core)
 
+    grad_in = pltpu.make_async_copy(grad_hbm, grad, local_sem.at[2])
+    grad_in.start()
+
     barrier = pltpu.get_barrier_semaphore()
 
     @pl.loop(1, NM)
@@ -147,6 +151,7 @@
         def _(k):
             b_copy(c, k).start()
 
+    grad_in.wait()
     pack(0)
     pl.semaphore_wait(barrier, NM - 1 + NZ - 1)
 
@@ -208,10 +213,6 @@
             rs_step(s)
 
     own = rows_of(0)
-    for chain in chains:
-        _, way, h, _ = chain
-        rs_copy(chain, 7, (rup if way == 1 else rdn).at[7, :, halves[h]]).wait_recv()
-    yall[own, :] = ypart[own, :] + rup[7] + rdn[7]
 
     def ag_copy(chain, s):
         name, way, h, _ = chain
@@ -238,7 +239,7 @@
         return pltpu.make_async_remote_copy(
             src_ref=src, dst_ref=dst, send_sem=send_sem, recv_sem=recv_sem, device_id=sibling, device_id_type=MESH)
 
-    g_pair = to_sibling(gown.at[1 - core], gsib, pair_send.at[0], pair_recv.at[0])
+    g_pair = to_sibling(yall.at[own], ysib, pair_send.at[0], pair_recv.at[0])
     w_pair = to_sibling(wpart.at[:, 1 - core], wsib, pair_send.at[1], pair_recv.at[1])
 
     def plane_copy(k, src, dst, send_sem, recv_sem):
@@ -252,40 +253,61 @@
             device_id=at_z((z + k) % NZ), device_id_type=MESH)
 
     def gram_1():
-        y = yall[own, :]
-        rhs[pl.ds(0, BLK), :] = y
+        g_pair.start()
+        rhs[pl.ds(0, BLK), :] = yall[own, :]
         rhs[pl.ds(BLK, WIDE), :] = jnp.zeros((WIDE, RANK), F32)
-        gram = lax.dot_general(y, y, TDOT, precision=HIGHEST, preferred_element_type=F32)
-        gown[...] = gram.reshape(2, NCHIP, NZ, RANK)
-        g_pair.start()
 
     def gram_2():
         g_pair.wait()
-        gsib[...] += gown[core]
+        y = jnp.concatenate([yall[own, :], ysib[...]], axis=0)
+
+        def blocks(i, first, count):
+            return lax.dot_general(
+                y[:, i * NB : (i + 1) * NB], y[:, first * NB : (first + count) * NB], TDOT,
+                precision=HIGHEST, preferred_element_type=F32).reshape(NCHIP, GR, count * NB)
+
+        @pl.when(core == 0)
+        def _():
+            gown[:, :, : 4 * NB] = blocks(0, 0, 4)
+            gown[:, :, 4 * NB :] = blocks(1, 1, 1)
+
+        @pl.when(core == 1)
+        def _():
+            gown[:, :, : 2 * NB] = blocks(1, 2, 2)
+            gown[:, :, 2 * NB : 4 * NB] = blocks(2, 2, 2)
+            gown[:, :, 4 * NB :] = blocks(3, 3, 1)
 
         @pl.loop(1, NCHIP)
         def _(k):
-            plane_copy(k, gsib.at[(chip + k) % NCHIP], grecv.at[chip], g_send, g_recv).start()
-
-        grecv[chip] = gsib[chip]
+            plane_copy(k, gown.at[(chip + k) % NCHIP], grecv.at[chip], g_send, g_recv).start()
+
+        grecv[chip] = gown[chip]
 
     def gram_3():
         await_bytes(grecv.at[pl.ds(0, NCHIP - 1)], g_recv)
-        gzs[...] = jnp.sum(grecv[...], axis=0).reshape(NZ, 1, RANK)
+        gzs[...] = jnp.sum(grecv[...], axis=0).reshape(GR, 1, GL)
 
         @pl.loop(1, NZ)
         def _(k):
-            z_copy(k, gzs.at[(z + k) % NZ], gzr.at[z], gzs_send, gzs_recv).start()
-
-        gzr[z] = gzs[z]
+            peer = (z + k) % NZ
+
+            @pl.when(peer < GR)
+            def _():
+                z_copy(k, gzs.at[peer], gzr.at[z], gzs_send, gzs_recv).start()
+
+        @pl.when(z < GR)
+        def _():
+            gzr[z] = gzs[z]
 
     def gram_4():
-        await_bytes(gzr.at[pl.ds(0, NZ - 1)], gzs_recv)
-        gza[z] = jnp.sum(gzr[...], axis=0)
-
-        @pl.loop(1, NZ)
-        def _(k):
-            z_copy(k, gza.at[z], gza.at[z], gza_send, gza_recv).start()
+        @pl.when(z < GR)
+        def _():
+            await_bytes(gzr.at[pl.ds(0, NZ - 1)], gzs_recv)
+            gza[z] = jnp.sum(gzr[...], axis=0)
+
+            @pl.loop(1, NZ)
+            def _(k):
+                z_copy(k, gza.at[z], gza.at[z], gza_send, gza_recv).start()
 
     def gp_copy(k):
         piece = gall.at[core, chip]
@@ -296,8 +318,15 @@
         return to_sibling(piece, piece, gs_send.at[k], gs_recv.at[k])
 
     def gram_5():
-        await_bytes(gza.at[pl.ds(0, NZ - 1)], gza_recv)
-        gall[core, chip] = gza[...].reshape(NZ, RANK)
+        @pl.when(z < GR)
+        def _():
+            await_bytes(gza.at[pl.ds(0, GR - 1)], gza_recv)
+
+        @pl.when(z >= GR)
+        def _():
+            await_bytes(gza, gza_recv)
+
+        gall[core, chip] = gza[...].reshape(GR, GL)
 
         @pl.loop(1, NCHIP)
         def _(k):
@@ -318,8 +347,8 @@
             piece = gall.at[1 - core, mod(chip - k, NCHIP)]
             to_sibling(piece, piece, gs_send.at[k], gs_recv.at[k]).wait_recv()
 
-    def gather_step(s):
-        for chain in chains:
+    def gather_step(s, which):
+        for chain in which:
             if s < 8 - chain[3]:
                 if s:
                     ag_copy(chain, s - 1).wait_recv()
@@ -329,23 +358,31 @@
         for chain in chains:
             ag_copy(chain, 7 - chain[3]).wait_recv()
 
-    gather_step(0)
+    for h in range(2):
+        ends = [chain for chain in chains if chain[2] == h]
+        for chain in ends:
+            rs_copy(chain, 7, (rup if chain[1] == 1 else rdn).at[7, :, halves[h]]).wait_recv()
+        yall[own, halves[h]] = ypart[own, halves[h]] + rup[7, :, halves[h]] + rdn[7, :, halves[h]]
+        gather_step(0, ends)
     gram_1()
-    gather_step(1)
+    one, two = chains[:2], chains[2:]
     gram_2()
-    gather_step(2)
+    gather_step(1, chains)
+    gather_step(2, chains)
     gram_3()
-    gather_step(3)
+    gather_step(3, chains)
     gram_4()
+    gather_step(4, one)
     use(3)
-    gather_step(4)
+    gather_step(4, two)
     gram_5()
     use(2)
-    gather_step(5)
+    gather_step(5, chains)
     gram_6()
-    gather_step(6)
+    gather_step(6, one)
+    gram_7()
+    gather_step(6, two)
     use(1)
-    gram_7()
 
     def w_send_off():
         w_pair.wait()
@@ -375,26 +412,33 @@
         def _():
             work_beside()
 
-    mat[:, :RANK] = gall[...].reshape(RANK, RANK)
+    upper_blocks = [gall[i].reshape(NB, GL) for i in range(2)]
+    mat[:, :RANK] = jnp.zeros((RANK, RANK), F32)
+    mat[below(0), :RANK] = upper_blocks[0][:, :RANK]
+    mat[below(1), NB : 2 * NB] = upper_blocks[0][:, RANK:]
+    mat[below(1), 2 * NB : RANK] = upper_blocks[1][:, : 2 * NB]
+    mat[below(2), 2 * NB : RANK] = upper_blocks[1][:, 2 * NB : 4 * NB]
+    mat[below(3), 3 * NB : RANK] = upper_blocks[1][:, 4 * NB :]
     mat[:, RANK:] = rhs[...].T
 
     @pl.loop(0, RANK // NB)
     def _(j):
         rows = pl.ds(pl.multiple_of(j * NB, NB), NB)
         work[...] = mat[rows, rows]
-
-        def halfway():
-            at(j, 0, lambda: gather_step(7))
-            at(j, 2, w_send_off)
-
-        invert_factor(work, halfway)
+        at(j, 1, lambda: gather_step(7, chains))
 
         def last_of_w():
             gather_end()
             use(0)
             w_pair.start()
 
-        at(j, 1, last_of_w)
+        at(j, 2, last_of_w)
+
+        def halfway():
+            at(j, 2, w_send_off)
+
+        invert_factor(work, halfway)
+
         row = lax.broadcasted_iota(jnp.int32, (NB, NB), 0)
         lane = lax.broadcasted_iota(jnp.int32, (NB, NB), 1)
         inverse = jnp.where(lane <= row, work[...], 0.0)
@@ -428,7 +472,7 @@
     for k in range(1, NX):
         x_copy(k).start()
     inbox_x[x] = outbox[:, x]
-    basis_out[...] = (solved[:, :BLK] * math.sqrt(ROWS)).astype(BF16)
+    basis_out[...] = (solved[...].T[:BLK] * math.sqrt(ROWS)).astype(BF16)
     for k in range(1, NX):
         x_copy(k).wait()
 
@@ -440,9 +484,17 @@
 
     for ref, sem in (
         (grecv.at[pl.ds(0, NCHIP - 1)], g_send), (wrecv.at[pl.ds(0, NCHIP - 1)], w_send),
-        (gzr.at[pl.ds(0, NZ - 1)], gzs_send), (gza.at[pl.ds(0, NZ - 1)], gza_send),
     ):
         await_bytes(ref, sem)
+
+    @pl.when(z < GR)
+    def _():
+        await_bytes(gza.at[pl.ds(0, GR - 1)], gzs_send)
+        await_bytes(gzr.at[pl.ds(0, NZ - 1)], gza_send)
+
+    @pl.when(z >= GR)
+    def _():
+        await_bytes(gza, gzs_send)
 
     @pl.loop(0, NCHIP)
     def _(k):
@@ -482,12 +534,13 @@
     return pl.pallas_call(
         kernel,
         out_shape=(
-            jax.ShapeDtypeStruct((RANK, BLK), BF16),
+            jax.ShapeDtypeStruct((BLK, RANK), BF16),
             jax.ShapeDtypeStruct((PER_DP, N_DP * WIDE), BF16),
         ),
-        in_specs=[vmem, pl.BlockSpec(memory_space=pl.ANY)],
+        in_specs=[pl.BlockSpec(memory_space=pl.ANY)] * 2,
         out_specs=(vmem, vmem),
         scratch_shapes=[
+            pltpu.VMEM((WIDE, ROWS), BF16),
             pltpu.VMEM((NM, WIDE, COLS), BF16),
             pltpu.VMEM((PW, COLS), BF16),
             pltpu.VMEM((NX, NT, WIDE, RANK), BF16),
@@ -498,13 +551,13 @@
             pltpu.VMEM((NCHIP, 2, WIDE, RANK), F32),
             pltpu.VMEM((NCHIP, WIDE, RANK), F32),
             pltpu.VMEM((NCHIP, WIDE, RANK), F32),
-            pltpu.VMEM((2, NCHIP, NZ, RANK), F32),
-            pltpu.VMEM((NCHIP, NZ, RANK), F32),
-            pltpu.VMEM((NCHIP, NZ, RANK), F32),
-            pltpu.VMEM((NZ, 1, RANK), F32),
-            pltpu.VMEM((NZ, 1, RANK), F32),
-            pltpu.VMEM((NZ, 1, RANK), F32),
-            pltpu.VMEM((2, NCHIP, NZ, RANK), F32),
+            pltpu.VMEM((BLK, RANK), F32),
+            pltpu.VMEM((NCHIP, GR, GL), F32),
+            pltpu.VMEM((NCHIP, GR, GL), F32),
+            pltpu.VMEM((GR, 1, GL), F32),
+            pltpu.VMEM((NZ, 1, GL), F32),
+            pltpu.VMEM((GR, 1, GL), F32),
+            pltpu.VMEM((2, NCHIP, GR, GL), F32),
             pltpu.VMEM((BLK + WIDE, RANK), F32),
             pltpu.VMEM((RANK, RANK + NB), F32),
             pltpu.VMEM((NB, NB), F32),
@@ -513,7 +566,7 @@
             pltpu.VMEM((NZ, NX, 1, NB), F32),
             pltpu.VMEM((NX, NZ, 1, NB), F32),
             pltpu.VMEM((NZ, NX, 1, NB), F32),
-            dma((2,)),
+            dma((3,)),
             dma((len(STEPS),)), dma((len(STEPS),)),
             dma((NT,)), dma((NT,)),
             dma((4, 8)), dma((4, 8)),
@@ -531,7 +584,8 @@
 
 
 def shards(grad_buckets, sketch):
-    return project(grad_buckets, sketch.reshape(NZ, NX, WIDE, RANK))
+    basis, projected = project(grad_buckets, sketch.reshape(NZ, NX, WIDE, RANK))
+    return basis.T, projected
 
 
 def solution(mesh):

time: 155 us -> 154 us (level)
    pallas_call x1 -> x0, local copies, waits for them, and re-layouts: 1.65 us -> none  [project(): pl.pallas_call(kernel, out_shape=(jax.ShapeDtypeStruct((RANK, BLK), BF16)...]
    unnamed x1 -> x2, local copies, waits for them, and re-layouts: 1.32 us -> 2.87 us
where the time goes in v6:
time: 154 us
  Pallas kernels  151 us (98%)
  local copies, waits for them, and re-layouts  2.87 us (2%)
    pallas_call x1, Pallas kernels, project(): pl.pallas_call(kernel, out_shape=(jax.ShapeDtypeStruct((BLK, RANK), BF16)...  151 us

profile of v6, /device:TPU:24, one launch (start us, length us, event | category | flops | bytes accessed | tf_op | source)
XLA Modules:
  0.0 154.2 jit_solution(3687703425360228941)
XLA Ops:
  0.6 150.7 %shard_map.41 = (bf16[112,512]{1,0:T(8,128)(2,1)}, bf16[8,1024]{1,0:T(8,128)(2,1)}) custom-call(bf16[16,57344]{1,0:T(8,128)(2,1)} %grad_hbm.1, bf16[16,4,16,512]{3,2,1,0:T(8,128)(2,1)} %bitcast.2), custom_call_target="tpu_custom_call" | custom-call | tf_op jit(solution)/shard_map/pallas_call | solution.py:534
  151.3 1.6 %copy.6 = bf16[512,112]{0,1:T(8,128)(2,1)} copy(bf16[512,112]{0,1:T(8,128)(2,1)} %bitcast.3) | data formatting | bytes 229376
  152.9 1.3 copy.7

commit v7 on v6

--- a/solution.py
+++ b/solution.py
@@ -82,7 +82,7 @@
 def kernel(
     grad_hbm, sketch, basis_out, proj_out,
     grad, packed, recv_b, recv_s, ypart, yall, rup, rdn, wpart, wsib, wrecv,
-    ysib, gown, grecv, gzs, gzr, gza, gall, rhs, mat, work, inverses, solved, outbox, inbox_x, inbox_z,
+    ysib, gown, grecv, gzs, gzr, gza, gall, rhs, mat, work, inverses, solved, solved_w, outbox, inbox_x, inbox_z,
     local_sem, a2a_send, a2a_recv, s_send, s_recv, rs_send, rs_recv, ag_send, ag_recv,
     pair_send, pair_recv, w_send, w_recv, g_send, g_recv, gzs_send, gzs_recv, gza_send, gza_recv,
     gp_send, gp_recv, gs_send, gs_recv, x_send, x_recv, z_send, z_recv,
@@ -136,12 +136,27 @@
             send_sem=a2a_send.at[c], recv_sem=a2a_recv.at[c], device_id=member(peer), device_id_type=MESH,
         )
 
-    def s_copy(k):
-        peer = (t + k) % NT
-        return pltpu.make_async_remote_copy(
-            src_ref=sketch.at[z], dst_ref=recv_s.at[:, t],
-            send_sem=s_send.at[k], recv_sem=s_recv.at[k], device_id=(dp, peer), device_id_type=MESH,
+    halves = (pl.ds(0, HALF), pl.ds(HALF, HALF))
+
+    def s_y(h, d):
+        return pltpu.make_async_remote_copy(
+            src_ref=sketch.at[z, :, :, halves[h]], dst_ref=recv_s.at[:, t, :, halves[h]],
+            send_sem=s_send.at[h, d], recv_sem=s_recv.at[h, d],
+            device_id=(dp, (t + 2 * d) % NT), device_id_type=MESH,
         )
+
+    def s_sibling(h, d):
+        piece = recv_s.at[:, mod(t - 2 * d, NT), :, halves[h]]
+        return pltpu.make_async_remote_copy(
+            src_ref=sketch.at[z, :, :, halves[h]] if d == 0 else piece, dst_ref=piece,
+            send_sem=s_send.at[h, NT // 2 + d], recv_sem=s_recv.at[h, NT // 2 + d],
+            device_id=sibling, device_id_type=MESH,
+        )
+
+    def s_forward(h):
+        for d in range(1, NT // 2):
+            s_y(h, d).wait_recv()
+            s_sibling(h, d).start()
 
     own_s = pltpu.make_async_copy(sketch.at[z], recv_s.at[:, t], local_sem.at[0])
     own_s.start()
@@ -155,13 +170,15 @@
     pack(0)
     pl.semaphore_wait(barrier, NM - 1 + NZ - 1)
 
-    @pl.loop(1, NT)
-    def _(k):
-        s_copy(k).start()
-
+    for h in range(2):
+        for d in range(1, NT // 2):
+            s_y(h, d).start()
+        s_sibling(h, 0).start()
     send(0)
+    pack(1)
+    s_forward(0)
     send(1)
-    pack(1)
+    s_forward(1)
     pack(2)
     pack(3)
 
@@ -170,14 +187,9 @@
     own_b.wait()
     own_s.wait()
 
-    @pl.loop(1, NT)
-    def _(k):
-        s_copy(k).wait()
-
     def rows_of(k):
         return pl.ds(near(k) * BLK, BLK)
 
-    halves = (pl.ds(0, HALF), pl.ds(HALF, HALF))
     chains = ((0, 1, 0, 0), (1, -1, 1, 0), (2, 1, 1, 1), (3, -1, 0, 1))
 
     def rs_copy(chain, s, src):
@@ -188,13 +200,17 @@
             send_sem=rs_send.at[name, s], recv_sem=rs_recv.at[name, s],
             device_id=zup if way == 1 else zdn, device_id_type=MESH,
         )
+
+    def rs_first(chain):
+        _, way, h, s = chain
+        rs_copy(chain, s, ypart.at[rows_of(way * (8 - s)), halves[h]]).start()
 
     def rs_step(s):
         for chain in chains:
             _, way, h, first = chain
             rows = rows_of(way * (8 - s))
             if s == first:
-                rs_copy(chain, s, ypart.at[rows, halves[h]]).start()
+                rs_first(chain)
             elif s > first:
                 buf = rup if way == 1 else rdn
                 slot = buf.at[s - 1, :, halves[h]]
@@ -207,10 +223,19 @@
         await_bytes(recv_b.at[pl.ds(0, (NM - 1) * WIDE), lanes], a2a_recv.at[c])
         if 0 < c < len(STEPS) - 1:
             send(c + 1)
-        ypart[lanes, :] = lax.dot_general(
-            recv_b[:, lanes], recv_s[...].reshape(PW, RANK), TDOT, preferred_element_type=F32)
-        for s in STEPS[c]:
-            rs_step(s)
+        if c == 0:
+            for h in range(2):
+                for d in range(NT // 2):
+                    s_sibling(h, d).wait_recv()
+                ypart[lanes, halves[h]] = lax.dot_general(
+                    recv_b[:, lanes], recv_s[:, :, :, halves[h]].reshape(PW, HALF), TDOT,
+                    preferred_element_type=F32)
+                rs_first(chains[h])
+        else:
+            ypart[lanes, :] = lax.dot_general(
+                recv_b[:, lanes], recv_s[...].reshape(PW, RANK), TDOT, preferred_element_type=F32)
+            for s in STEPS[c]:
+                rs_step(s)
 
     own = rows_of(0)
 
@@ -399,13 +424,17 @@
 
     def w_solve():
         await_bytes(wrecv.at[pl.ds(0, NCHIP - 1)], w_recv)
-        w = jnp.concatenate([jnp.zeros((BLK, RANK), F32), jnp.sum(wrecv[...], axis=0)], axis=0).T
+        w = jnp.sum(wrecv[...], axis=0)
+        parts = []
         for j in range(RANK // NB):
-            part = jnp.dot(inverses[j], w[:NB], precision=HIGHEST, preferred_element_type=F32)
-            solved[below(j), :] += part
+            part = lax.dot_general(
+                w[:, :NB], inverses[j], (((1,), (1,)), ((), ())), precision=HIGHEST, preferred_element_type=F32)
+            parts.append(part)
             if j + 1 < RANK // NB:
-                w = w[NB:] - lax.dot_general(
-                    mat[below(j), (j + 1) * NB : RANK], part, TDOT, precision=HIGHEST, preferred_element_type=F32)
+                w = w[:, NB:] - jnp.dot(
+                    part, mat[below(j), (j + 1) * NB : RANK], precision=HIGHEST, preferred_element_type=F32)
+        rhs[pl.ds(BLK, WIDE), :] = jnp.concatenate(parts, axis=1)
+        solved_w[...] = rhs[...].T
 
     def at(j, now, work_beside):
         @pl.when(j == now)
@@ -457,7 +486,7 @@
     packed_p = jnp.zeros((N_DP, NB), F32)
     lane = lax.broadcasted_iota(jnp.int32, (N_DP, NB), 1)
     for r in range(PER_DP):
-        part = solved[pl.ds(r, N_DP, stride=PER_DP), :]
+        part = solved_w[pl.ds(r, N_DP, stride=PER_DP), :]
         slot = PER_DP - 1 - r
         packed_p = jnp.where(lane // WIDE == slot, pltpu.roll(part, (WIDE * slot - BLK) % NB, 1), packed_p)
     outbox[...] = packed_p.reshape(NZ, NX, 1, NB)
@@ -481,6 +510,12 @@
         z_copy(k, inbox_x.at[:, (z + k) % NZ], inbox_z.at[z], z_send, z_recv).start()
 
     inbox_z[z] = inbox_x[:, z]
+
+    for h in range(2):
+        for d in range(NT // 2):
+            s_sibling(h, d).wait_send()
+        for d in range(1, NT // 2):
+            s_y(h, d).wait_send()
 
     for ref, sem in (
         (grecv.at[pl.ds(0, NCHIP - 1)], g_send), (wrecv.at[pl.ds(0, NCHIP - 1)], w_send),
@@ -563,12 +598,13 @@
             pltpu.VMEM((NB, NB), F32),
             pltpu.VMEM((RANK // NB, NB, NB), F32),
             pltpu.VMEM((RANK, NB), F32),
+            pltpu.VMEM((RANK, NB), F32),
             pltpu.VMEM((NZ, NX, 1, NB), F32),
             pltpu.VMEM((NX, NZ, 1, NB), F32),
             pltpu.VMEM((NZ, NX, 1, NB), F32),
             dma((3,)),
             dma((len(STEPS),)), dma((len(STEPS),)),
-            dma((NT,)), dma((NT,)),
+            dma((2, NT)), dma((2, NT)),
             dma((4, 8)), dma((4, 8)),
             dma((4, 8)), dma((4, 8)),
             dma((2,)), dma((2,)),

time: 154 us -> 153 us (level)
  Pallas kernels: 151 us -> 149 us
    pallas_call x1, Pallas kernels: 151 us -> 149 us  [project(): pl.pallas_call(kernel, out_shape=(jax.ShapeDtypeStruct((BLK, RANK), BF16)...]
where the time goes in v7:
time: 153 us; the launch traced here: 152 us
  Pallas kernels  149 us (97%)
  local copies, waits for them, and re-layouts  2.87 us (2%)
    pallas_call x1, Pallas kernels, project(): pl.pallas_call(kernel, out_shape=(jax.ShapeDtypeStruct((BLK, RANK), BF16)...  149 us

profile of v7, /device:TPU:24, one launch (start us, length us, event | category | flops | bytes accessed | tf_op | source)
XLA Modules:
  0.0 152.4 jit_solution(2144299197580580991)
XLA Ops:
  0.6 148.9 %shard_map.41 = (bf16[112,512]{1,0:T(8,128)(2,1)}, bf16[8,1024]{1,0:T(8,128)(2,1)}) custom-call(bf16[16,57344]{1,0:T(8,128)(2,1)} %grad_hbm.1, bf16[16,4,16,512]{3,2,1,0:T(8,128)(2,1)} %bitcast.2), custom_call_target="tpu_custom_call" | custom-call | tf_op jit(solution)/shard_map/pallas_call | solution.py:569
  149.5 1.6 %copy.6 = bf16[512,112]{0,1:T(8,128)(2,1)} copy(bf16[512,112]{0,1:T(8,128)(2,1)} %bitcast.3) | data formatting | bytes 229376
  151.1 1.3 copy.7

commit v8 on v7

--- a/solution.py
+++ b/solution.py
@@ -45,6 +45,10 @@
 
 
 ORDER = sorted(range(1 - NZ // 2, NZ // 2 + 1), key=near)
+
+
+def far_first(i):
+    return NZ // 2 + (i // 2) * (2 * (i % 2) - 1)
 
 
 def await_bytes(ref, sem):
@@ -308,12 +312,52 @@
 
         grecv[chip] = gown[chip]
 
+    def left_early():
+        for h in range(2):
+            for d in range(NT // 2):
+                s_sibling(h, d).wait_send()
+            for d in range(1, NT // 2):
+                s_y(h, d).wait_send()
+        for c in range(len(STEPS)):
+            await_bytes(recv_b.at[pl.ds(0, (NM - 1) * WIDE), pl.ds(PARTS[c], PARTS[c + 1] - PARTS[c])], a2a_send.at[c])
+        for chain in chains:
+            for s in range(chain[3], 8):
+                rs_copy(chain, s, (rup if chain[1] == 1 else rdn).at[s, :, halves[chain[2]]]).wait_send()
+
+    def left_late():
+        for ref, sem in (
+            (grecv.at[pl.ds(0, NCHIP - 1)], g_send), (wrecv.at[pl.ds(0, NCHIP - 1)], w_send),
+        ):
+            await_bytes(ref, sem)
+
+        @pl.when(z < GR)
+        def _():
+            await_bytes(gza.at[pl.ds(0, GR - 1)], gzs_send)
+            await_bytes(gzr.at[pl.ds(0, NZ - 1)], gza_send)
+
+        @pl.when(z >= GR)
+        def _():
+            await_bytes(gza, gzs_send)
+
+        @pl.loop(0, NCHIP)
+        def _(k):
+            gs_copy(k).wait_send()
+
+        @pl.loop(1, NCHIP)
+        def _(k):
+            gp_copy(k).wait_send()
+
+        for chain in chains:
+            for s in range(0, 8 - chain[3]):
+                ag_copy(chain, s).wait_send()
+
     def gram_3():
         await_bytes(grecv.at[pl.ds(0, NCHIP - 1)], g_recv)
         gzs[...] = jnp.sum(grecv[...], axis=0).reshape(GR, 1, GL)
 
         @pl.loop(1, NZ)
-        def _(k):
+        def _(i):
+            k = far_first(i)
             peer = (z + k) % NZ
 
             @pl.when(peer < GR)
@@ -331,7 +375,8 @@
             gza[z] = jnp.sum(gzr[...], axis=0)
 
             @pl.loop(1, NZ)
-            def _(k):
+            def _(i):
+                k = far_first(i)
                 z_copy(k, gza.at[z], gza.at[z], gza_send, gza_recv).start()
 
     def gp_copy(k):
@@ -393,6 +438,7 @@
     one, two = chains[:2], chains[2:]
     gram_2()
     gather_step(1, chains)
+    left_early()
     gather_step(2, chains)
     gram_3()
     gather_step(3, chains)
@@ -481,6 +527,8 @@
                 mat[below(i), :] -= lax.dot_general(
                     upper[:, i * NB : (i + 1) * NB], upper, TDOT, precision=HIGHEST, preferred_element_type=F32)
 
+    basis_out[...] = (solved[...].T[:BLK] * math.sqrt(ROWS)).astype(BF16)
+    left_late()
     w_solve()
 
     packed_p = jnp.zeros((N_DP, NB), F32)
@@ -501,52 +549,15 @@
     for k in range(1, NX):
         x_copy(k).start()
     inbox_x[x] = outbox[:, x]
-    basis_out[...] = (solved[...].T[:BLK] * math.sqrt(ROWS)).astype(BF16)
     for k in range(1, NX):
         x_copy(k).wait()
 
     @pl.loop(1, NZ)
-    def _(k):
+    def _(i):
+        k = far_first(i)
         z_copy(k, inbox_x.at[:, (z + k) % NZ], inbox_z.at[z], z_send, z_recv).start()
 
     inbox_z[z] = inbox_x[:, z]
-
-    for h in range(2):
-        for d in range(NT // 2):
-            s_sibling(h, d).wait_send()
-        for d in range(1, NT // 2):
-            s_y(h, d).wait_send()
-
-    for ref, sem in (
-        (grecv.at[pl.ds(0, NCHIP - 1)], g_send), (wrecv.at[pl.ds(0, NCHIP - 1)], w_send),
-    ):
-        await_bytes(ref, sem)
-
-    @pl.when(z < GR)
-    def _():
-        await_bytes(gza.at[pl.ds(0, GR - 1)], gzs_send)
-        await_bytes(gzr.at[pl.ds(0, NZ - 1)], gza_send)
-
-    @pl.when(z >= GR)
-    def _():
-        await_bytes(gza, gzs_send)
-
-    @pl.loop(0, NCHIP)
-    def _(k):
-        gs_copy(k).wait_send()
-
-    @pl.loop(1, NCHIP)
-    def _(k):
-        gp_copy(k).wait_send()
-
-    for c in range(len(STEPS)):
-        await_bytes(recv_b.at[pl.ds(0, (NM - 1) * WIDE), pl.ds(PARTS[c], PARTS[c + 1] - PARTS[c])], a2a_send.at[c])
-    for chain in chains:
-        _, way, h, first = chain
-        for s in range(first, 8):
-            rs_copy(chain, s, (rup if way == 1 else rdn).at[s, :, halves[h]]).wait_send()
-        for s in range(0, 8 - first):
-            ag_copy(chain, s).wait_send()
 
     await_bytes(inbox_z.at[pl.ds(0, NZ - 1)], z_send)
     await_bytes(inbox_z.at[pl.ds(0, NZ - 1)], z_recv)

time: 153 us -> 152 us (level)
  no operation moved by 1% of the time
where the time goes in v8:
time: 152 us
  Pallas kernels  148 us (97%)
  local copies, waits for them, and re-layouts  2.87 us (2%)
    pallas_call x1, Pallas kernels, project(): pl.pallas_call(kernel, out_shape=(jax.ShapeDtypeStruct((BLK, RANK), BF16)...  148 us

profile of v8, /device:TPU:24, one launch (start us, length us, event | category | flops | bytes accessed | tf_op | source)
XLA Modules:
  0.0 151.7 jit_solution(6204159230592264123)
XLA Ops:
  0.6 148.2 %shard_map.41 = (bf16[112,512]{1,0:T(8,128)(2,1)}, bf16[8,1024]{1,0:T(8,128)(2,1)}) custom-call(bf16[16,57344]{1,0:T(8,128)(2,1)} %grad_hbm.1, bf16[16,4,16,512]{3,2,1,0:T(8,128)(2,1)} %bitcast.2), custom_call_target="tpu_custom_call" | custom-call | tf_op jit(solution)/shard_map/pallas_call | solution.py:580
  148.8 1.6 %copy.6 = bf16[512,112]{0,1:T(8,128)(2,1)} copy(bf16[512,112]{0,1:T(8,128)(2,1)} %bitcast.3) | data formatting | bytes 229376
  150.4 1.3 copy.7

commit v9 on v8

--- a/solution.py
+++ b/solution.py
@@ -507,10 +507,10 @@
             use(0)
             w_pair.start()
 
-        at(j, 2, last_of_w)
+        at(j, 2, w_send_off)
 
         def halfway():
-            at(j, 2, w_send_off)
+            at(j, 1, last_of_w)
 
         invert_factor(work, halfway)
 

time: 152 us -> 152 us (level)
  no operation moved by 1% of the time
where the time goes in v9:
time: 152 us; the launch traced here: 151 us
  Pallas kernels  148 us (97%)
  local copies, waits for them, and re-layouts  2.87 us (2%)
    pallas_call x1, Pallas kernels, project(): pl.pallas_call(kernel, out_shape=(jax.ShapeDtypeStruct((BLK, RANK), BF16)...  148 us

profile of v9, /device:TPU:24, one launch (start us, length us, event | category | flops | bytes accessed | tf_op | source)
XLA Modules:
  0.0 151.4 jit_solution(6601877025569187436)
XLA Ops:
  0.6 147.9 %shard_map.41 = (bf16[112,512]{1,0:T(8,128)(2,1)}, bf16[8,1024]{1,0:T(8,128)(2,1)}) custom-call(bf16[16,57344]{1,0:T(8,128)(2,1)} %grad_hbm.1, bf16[16,4,16,512]{3,2,1,0:T(8,128)(2,1)} %bitcast.2), custom_call_target="tpu_custom_call" | custom-call | tf_op jit(solution)/shard_map/pallas_call | solution.py:580
  148.6 1.6 %copy.6 = bf16[512,112]{0,1:T(8,128)(2,1)} copy(bf16[512,112]{0,1:T(8,128)(2,1)} %bitcast.3) | data formatting | bytes 229376
  150.1 1.3 copy.7
